TPU v7x, 32 devices: a whole 2x2x4 slice. The times are simulated.
32 devices in a mesh: pipe: 2 (over core), dp: 4 (over z), seq: 2 (over x), mp: 2 (over y).
Axes of the slice: x: 2, y: 2, z: 4, core: 2. Of those that a mesh axis runs over, the one named last changes fastest.
Arguments:
- characters: bfloat16 [16, 2048, 768], P('dp', ('seq', 'mp'), 'pipe'), may hold values from -6 to 6
- row_lengths: int32 [16], P('dp'), may hold values from 204 to 2048, as said below
- w_query: bfloat16 [768, 768], P(None, 'mp'), may hold values from -0.21875 to 0.21875
- b_query: bfloat16 [768], P('mp'), may hold values from -1.75 to 1.75
- w_key: bfloat16 [768, 768], P(None, 'mp'), may hold values from -0.21875 to 0.21875
- w_value: bfloat16 [768, 768], P(None, 'mp'), may hold values from -0.21875 to 0.21875
- b_value: bfloat16 [768], P('mp'), may hold values from -1.75 to 1.75
- w_attn_out: bfloat16 [768, 768], P('mp'), may hold values from -0.875 to 0.875
- b_attn_out: bfloat16 [768], replicated, may hold values from -1.75 to 1.75
- gain_one: bfloat16 [768], replicated, may hold values from 0.5 to 1.5
- shift_one: bfloat16 [768], replicated, may hold values from -1.75 to 1.75
- w_inner: bfloat16 [768, 3072], P(None, 'mp'), may hold values from -0.21875 to 0.21875
- b_inner: bfloat16 [3072], P('mp'), may hold values from -1.75 to 1.75
- w_outer: bfloat16 [3072, 768], P('mp'), may hold values from -0.15625 to 0.15625
- b_outer: bfloat16 [768], replicated, may hold values from -1.75 to 1.75
- gain_two: bfloat16 [768], replicated, may hold values from 0.5 to 1.5
- shift_two: bfloat16 [768], replicated, may hold values from -1.75 to 1.75
- w_conv: bfloat16 [3072, 768], replicated, may hold values from -0.109375 to 0.109375
- b_conv: bfloat16 [768], replicated, may hold values from -1.75 to 1.75
- gain_three: bfloat16 [768], replicated, may hold values from 0.5 to 1.5
- shift_three: bfloat16 [768], replicated, may hold values from -1.75 to 1.75
- molecule_grad: bfloat16 [16, 512, 768], P('dp', ('seq', 'mp'), 'pipe'), may hold values from -6 to 6
Outputs:
- molecules: bfloat16 [16, 512, 768], P('dp', ('seq', 'mp'), 'pipe')
- chars_grad: float32 [16, 2048, 768], P('dp', ('seq', 'mp'), 'pipe')
- grad_w_query: float32 [768, 768], P(('pipe', 'dp', 'seq'), 'mp')
- grad_b_query: float32 [768], replicated
- grad_w_key: float32 [768, 768], P(('pipe', 'dp', 'seq'), 'mp')
- grad_w_value: float32 [768, 768], P(('pipe', 'dp', 'seq'), 'mp')
- grad_b_value: float32 [768], replicated
- grad_w_attn_out: float32 [768, 768], P('mp', ('pipe', 'dp', 'seq'))
- grad_b_attn_out: float32 [768], replicated
- grad_gain_one: float32 [768], replicated
- grad_shift_one: float32 [768], replicated
- grad_w_inner: float32 [768, 3072], P(('pipe', 'dp', 'seq'), 'mp')
- grad_b_inner: float32 [3072], replicated
- grad_w_outer: float32 [3072, 768], P('mp', ('pipe', 'dp', 'seq'))
- grad_b_outer: float32 [768], replicated
- grad_gain_two: float32 [768], replicated
- grad_shift_two: float32 [768], replicated
- grad_w_conv: float32 [3072, 768], P(('pipe', 'dp', 'seq', 'mp'))
- grad_b_conv: float32 [768], replicated
- grad_gain_three: float32 [768], replicated
- grad_shift_three: float32 [768], replicated
Inputs may be any that keep to these rules, and one draw needn't show every extreme that they name: `row_lengths`: each aligned block of 4 rows holds one row of length 2048.
All inputs are finite; a program needn't handle non-finite values.
Results may differ from a plain program's by a relative error of at most 0.023.
Values may be sent and summed in bfloat16 or wider, within the bound.
No kernel may reach another device: no remote copies, remote signals or barrier semaphores. Data moves between devices by JAX's collectives and lax.ppermute only.
A program may use at most 448 MiB of HBM per device.

v0:
```python
import jax
import jax.numpy as jnp
from jax import lax
from jax.sharding import PartitionSpec as P

HEAD = 64
WINDOW = 128
KERNEL = 4
MB = 4


epsilon = 1e-05
masked_score = -1e30


def passed_along(block, axis, distance):
    devices = range(lax.axis_size(axis))
    route = [(i - distance, i) for i in devices if i - distance in devices]
    return lax.ppermute(block, axis, route)


def with_halo(cells, sides, width):
    for axis, dim in sides:
        count = lax.axis_size(axis)
        ends = count - 1
        head = lax.slice_in_dim(cells, 0, width, axis=dim)
        tail = lax.slice_in_dim(cells, cells.shape[dim] - width, cells.shape[dim], axis=dim)
        cells = jnp.concatenate(
            [
                lax.ppermute(tail, axis, [(i, (i + 1) % count) for i in range(ends)]),
                cells,
                lax.ppermute(head, axis, [((i + 1) % count, i) for i in range(ends)]),
            ],
            axis=dim,
        )
    return cells


def normalize(values, gain, shift):
    centered = values - jnp.mean(values, axis=-1, keepdims=True)
    spread = jnp.mean(centered * centered, axis=-1, keepdims=True)
    return centered * lax.rsqrt(spread + epsilon) * gain + shift


def on_section(active, work):

    def skipped():
        return jax.tree.map(jnp.zeros_like, work())

    return lax.cond(active, work, skipped)


def run_section(active, work):
    return on_section(active, work)


def gather_halves(block_rows):
    return lax.all_gather(block_rows, "mp", axis=1, tiled=True)


def scatter_halves(block_terms):
    return lax.psum_scatter(
        block_terms.astype(jnp.bfloat16), "mp", scatter_dimension=1, tiled=True
    ).astype(jnp.float32)


def rows_product(left, right):
    return jnp.einsum("bsi,bsj->ij", left, right, preferred_element_type=jnp.float32)


def apply_right(left, right):
    return jnp.einsum("bsi,ij->bsj", left, right, preferred_element_type=jnp.float32)


def apply_transposed(left, right):
    return jnp.einsum("bsj,ij->bsi", left, right, preferred_element_type=jnp.float32)


def windowed(extended_part, blocks, head_count):
    row_count = extended_part.shape[0]
    shaped = extended_part.reshape(row_count, blocks + 2, WINDOW, head_count, HEAD)
    return jnp.concatenate([shaped[:, :-2], shaped[:, 1:-1], shaped[:, 2:]], axis=2)


def fold_windows(grads):
    pair_count, row_count, blocks = (grads.shape[0], grads.shape[1], grads.shape[2])
    pieces = grads.reshape(pair_count, row_count, blocks, 3, WINDOW, -1)
    left_part = jnp.pad(pieces[:, :, :, 0], ((0, 0), (0, 0), (0, 2), (0, 0), (0, 0)))
    middle_part = jnp.pad(pieces[:, :, :, 1], ((0, 0), (0, 0), (1, 1), (0, 0), (0, 0)))
    right_part = jnp.pad(pieces[:, :, :, 2], ((0, 0), (0, 0), (2, 0), (0, 0), (0, 0)))
    return (left_part + middle_part + right_part).reshape(
        pair_count, row_count, (blocks + 2) * WINDOW, -1
    )


def allowed_pairs(lengths, row_start, blocks):
    offsets = row_start + jnp.arange(blocks, dtype=jnp.int32)[:, None, None] * WINDOW
    query_pos = offsets + jnp.arange(WINDOW, dtype=jnp.int32)[None, :, None]
    key_pos = offsets - WINDOW + jnp.arange(3 * WINDOW, dtype=jnp.int32)[None, None, :]
    in_window = jnp.abs(query_pos - key_pos) < WINDOW
    return in_window[None] & (key_pos[None] >= 0) & (key_pos[None] < lengths[:, None, None, None])


def score_blocks(queries, extended, allowed):
    row_count = queries.shape[0]
    blocks = queries.shape[1] // WINDOW
    head_count = queries.shape[2] // HEAD
    shaped = queries.reshape(row_count, blocks, WINDOW, head_count, HEAD)
    key_win = windowed(extended[0], blocks, head_count)
    value_win = windowed(extended[1], blocks, head_count)
    scores = jnp.einsum(
        "bnqhe,bnkhe->bnhqk", shaped, key_win, preferred_element_type=jnp.float32
    ) * HEAD ** (-0.5)
    scores = jnp.where(allowed[:, :, None], scores, masked_score)
    return (shaped, key_win, value_win, scores)


def attention_forward(queries, extended, allowed):
    row_count, full_span, local_width = queries.shape
    shaped, key_win, value_win, scores = score_blocks(queries, extended, allowed)
    row_max = jnp.max(scores, axis=-1, keepdims=True)
    weights = jnp.exp(scores - row_max)
    row_total = jnp.sum(weights, axis=-1, keepdims=True)
    weights_low = (weights / row_total).astype(jnp.bfloat16)
    attended = jnp.einsum(
        "bnhqk,bnkhe->bnqhe", weights_low, value_win, preferred_element_type=jnp.float32
    )
    attended = attended.reshape(row_count, full_span, local_width).astype(jnp.bfloat16)
    return (attended, row_max + jnp.log(row_total))


def attention_backward(queries, extended, allowed, log_total, grad_attended):
    row_count, full_span, local_width = queries.shape
    shaped, key_win, value_win, scores = score_blocks(queries, extended, allowed)
    probs = jnp.exp(scores - log_total)
    grad_out = grad_attended.reshape(shaped.shape)
    grad_probs = jnp.einsum(
        "bnqhe,bnkhe->bnhqk", grad_out, value_win, preferred_element_type=jnp.float32
    )
    inner_sum = jnp.sum(probs * grad_probs, axis=-1, keepdims=True)
    grad_scores = jnp.where(allowed[:, :, None], probs * (grad_probs - inner_sum), 0.0).astype(
        jnp.bfloat16
    )
    scale = HEAD ** (-0.5)
    grad_queries = (
        jnp.einsum("bnhqk,bnkhe->bnqhe", grad_scores, key_win, preferred_element_type=jnp.float32)
        * scale
    )
    grad_key_win = (
        jnp.einsum("bnhqk,bnqhe->bnkhe", grad_scores, shaped, preferred_element_type=jnp.float32)
        * scale
    )
    grad_value_win = jnp.einsum(
        "bnhqk,bnqhe->bnkhe",
        probs.astype(jnp.bfloat16),
        grad_out,
        preferred_element_type=jnp.float32,
    )
    grad_padded = fold_windows(jnp.stack([grad_key_win, grad_value_win], axis=0))
    return (grad_queries.reshape(row_count, full_span, local_width), grad_padded)


def on_device(
    characters,
    row_lengths,
    w_query,
    b_query,
    w_key,
    w_value,
    b_value,
    w_attn_out,
    b_attn_out,
    gain_one,
    shift_one,
    w_inner,
    b_inner,
    w_outer,
    b_outer,
    gain_two,
    shift_two,
    w_conv,
    b_conv,
    gain_three,
    shift_three,
    molecule_grad,
):
    leading = lax.axis_index("pipe") == 0
    trailing = jnp.logical_not(leading)
    halves = lax.axis_size("mp")
    half_span = characters.shape[1]
    full_span = halves * half_span
    blocks = full_span // WINDOW
    row_start = lax.axis_index("seq") * full_span
    own_start = row_start + lax.axis_index("mp") * half_span
    micro_rows = characters.shape[0] // MB
    half_width = characters.shape[2]
    local_width = w_query.shape[1]
    mol_count = half_span // KERNEL
    norm_gain_one = gain_one.astype(jnp.float32)
    norm_shift_one = shift_one.astype(jnp.float32)
    norm_gain_two = gain_two.astype(jnp.float32)
    norm_shift_two = shift_two.astype(jnp.float32)
    norm_gain_three = gain_three.astype(jnp.float32)
    norm_shift_three = shift_three.astype(jnp.float32)
    upper_part = passed_along(characters, "pipe", -1)
    full_chars = jnp.concatenate([characters, upper_part], axis=2)
    step_count = MB
    w_joined = jnp.concatenate([w_query, w_key, w_value], axis=1)
    b_joined = jnp.concatenate(
        [
            b_query.astype(jnp.float32),
            jnp.zeros((local_width,), jnp.float32),
            b_value.astype(jnp.float32),
        ]
    )

    def widen(piece):
        zeros_full = jnp.zeros((piece.shape[0] * halves,), jnp.float32)
        return lax.dynamic_update_slice_in_dim(
            zeros_full, piece, lax.axis_index("mp") * piece.shape[0], 0
        )

    def micro_step(offset):
        tokens = full_chars[offset : offset + micro_rows]
        lengths = row_lengths[offset : offset + micro_rows]
        own_grad = molecule_grad[offset : offset + micro_rows]
        token_pos = own_start + jnp.arange(half_span, dtype=jnp.int32)
        live_rows = (token_pos[None, :] < lengths[:, None]).astype(jnp.float32)[:, :, None]
        mol_pos = (own_start // KERNEL + jnp.arange(mol_count, dtype=jnp.int32)) * KERNEL
        live_mols = (mol_pos[None, :] < lengths[:, None]).astype(jnp.float32)[:, :, None]
        allowed = allowed_pairs(lengths, row_start, blocks)
        gathered = gather_halves(tokens)

        def project_heads():
            return (apply_right(gathered, w_joined) + b_joined).astype(jnp.bfloat16)

        projected = run_section(leading, project_heads)
        queries = projected[:, :, :local_width]
        key_values = jnp.stack(
            [projected[:, :, local_width : 2 * local_width], projected[:, :, 2 * local_width :]],
            axis=0,
        )
        extended = with_halo(key_values, (("seq", 2),), WINDOW)

        def attend_local():
            attended, log_total = attention_forward(queries, extended, allowed)
            return (attended, log_total, apply_right(attended, w_attn_out))

        attended, log_total, attn_terms = run_section(leading, attend_local)
        attn_part = scatter_halves(attn_terms)

        def first_norm():
            before = tokens.astype(jnp.float32) + attn_part + b_attn_out.astype(jnp.float32)
            return (before, normalize(before, norm_gain_one, norm_shift_one))

        before_one, middle = run_section(leading, first_norm)
        middle_full = gather_halves(middle.astype(jnp.bfloat16))

        def feed_local():
            hidden = apply_right(middle_full, w_inner) + b_inner.astype(jnp.float32)
            activated = jax.nn.gelu(hidden, approximate=False).astype(jnp.bfloat16)
            return (hidden, apply_right(activated, w_outer))

        hidden, feed_terms = run_section(leading, feed_local)
        feed_part = scatter_halves(feed_terms)

        def second_norm():
            before = middle + feed_part + b_outer.astype(jnp.float32)
            sent_rows = (normalize(before, norm_gain_two, norm_shift_two) * live_rows).astype(
                jnp.bfloat16
            )
            return (before, sent_rows)

        before_two, sent_rows = run_section(leading, second_norm)
        arrived, grad_lower = passed_along((sent_rows, own_grad), "pipe", 1)
        cotangent = jnp.concatenate([grad_lower, own_grad], axis=2).astype(jnp.float32)

        def second_layer():
            grouped = arrived.reshape(micro_rows, mol_count, KERNEL * arrived.shape[2])
            conv_out = apply_right(grouped, w_conv) + b_conv.astype(jnp.float32)

            def finish(conv_value, gain, shift):
                return (
                    normalize(jax.nn.gelu(conv_value, approximate=False), gain, shift) * live_mols
                )

            mol_value, pullback = jax.vjp(finish, conv_out, norm_gain_three, norm_shift_three)
            grad_conv, grad_gain, grad_shift = pullback(cotangent)
            grad_low = grad_conv.astype(jnp.bfloat16)
            grad_w_conv = rows_product(grouped, grad_low)
            grad_b_conv = jnp.sum(grad_low.astype(jnp.float32), axis=(0, 1))
            grad_back = (
                apply_transposed(grad_low, w_conv).reshape(arrived.shape).astype(jnp.bfloat16)
            )
            return (
                mol_value.astype(jnp.bfloat16),
                grad_back,
                grad_w_conv,
                grad_b_conv,
                grad_gain,
                grad_shift,
            )

        mol_out, grad_sent, grad_w_conv, grad_b_conv, grad_gain_three, grad_shift_three = (
            run_section(trailing, second_layer)
        )
        grad_arrived, lower_out = passed_along((grad_sent, mol_out[:, :, :half_width]), "pipe", -1)
        mol_pieces = (lower_out, mol_out[:, :, half_width:])

        def second_back():

            def finish(pre_value, gain, shift):
                return normalize(pre_value, gain, shift) * live_rows

            pullback = jax.vjp(finish, before_two, norm_gain_two, norm_shift_two)[1]
            return pullback(grad_arrived.astype(jnp.float32))

        grad_two, grad_gain_two, grad_shift_two = run_section(leading, second_back)
        grad_feed_full = gather_halves(grad_two.astype(jnp.bfloat16))

        def feed_back():
            activated = jax.nn.gelu(hidden, approximate=False).astype(jnp.bfloat16)
            grad_activated = apply_transposed(grad_feed_full, w_outer)
            pullback = jax.vjp(
                lambda inner_value: jax.nn.gelu(inner_value, approximate=False), hidden
            )[1]
            grad_hidden = pullback(grad_activated)[0].astype(jnp.bfloat16)
            return (
                rows_product(activated, grad_feed_full),
                rows_product(middle_full, grad_hidden),
                jnp.sum(grad_hidden.astype(jnp.float32), axis=(0, 1)),
                apply_transposed(grad_hidden, w_inner),
            )

        grad_w_outer, grad_w_inner, grad_b_inner, middle_terms = run_section(leading, feed_back)
        middle_part = scatter_halves(middle_terms)

        def first_back():
            pullback = jax.vjp(normalize, before_one, norm_gain_one, norm_shift_one)[1]
            return pullback(grad_two + middle_part)

        grad_one, grad_gain_one, grad_shift_one = run_section(leading, first_back)
        grad_attn_full = gather_halves(grad_one.astype(jnp.bfloat16))

        def attention_back():
            grad_w_attn = rows_product(attended, grad_attn_full)
            grad_attended = apply_transposed(grad_attn_full, w_attn_out).astype(jnp.bfloat16)
            grad_queries, grad_padded = attention_backward(
                queries, extended, allowed, log_total, grad_attended
            )
            rim_grads = jnp.concatenate(
                [grad_padded[:, :, :WINDOW], grad_padded[:, :, -WINDOW:]], axis=2
            )
            return (grad_w_attn, grad_queries, grad_padded, rim_grads)

        grad_w_attn, grad_queries, grad_padded, rim_grads = run_section(leading, attention_back)
        returned = with_halo(rim_grads.astype(jnp.bfloat16), (("seq", 2),), WINDOW).astype(
            rim_grads.dtype
        )

        def projection_back():
            own_part = grad_padded[:, :, WINDOW:-WINDOW]
            pad_head = ((0, 0), (0, 0), (0, full_span - WINDOW), (0, 0))
            pad_tail = ((0, 0), (0, 0), (full_span - WINDOW, 0), (0, 0))
            head_rim = jnp.pad(returned[:, :, :WINDOW], pad_head)
            tail_rim = jnp.pad(returned[:, :, -WINDOW:], pad_tail)
            grad_kv = (own_part + head_rim + tail_rim).astype(jnp.bfloat16)
            grad_all = jnp.concatenate(
                [grad_queries.astype(jnp.bfloat16), grad_kv[0], grad_kv[1]], axis=2
            )
            return (
                rows_product(gathered, grad_all),
                jnp.sum(grad_all.astype(jnp.float32), axis=(0, 1)),
                apply_transposed(grad_all, w_joined),
            )

        grad_w_joined, grad_b_joined, input_terms = run_section(leading, projection_back)
        input_part = scatter_halves(input_terms)
        grad_tokens = input_part + grad_one
        head_terms = (grad_w_joined, grad_w_attn, grad_w_inner, grad_w_outer)
        vector_terms = (
            grad_b_joined[:local_width],
            grad_b_joined[2 * local_width :],
            jnp.sum(grad_one, axis=(0, 1)),
            grad_gain_one,
            grad_shift_one,
            grad_b_inner,
            jnp.sum(grad_two, axis=(0, 1)),
            grad_gain_two,
            grad_shift_two,
            grad_b_conv,
            grad_gain_three,
            grad_shift_three,
        )
        return (grad_tokens, mol_pieces, (head_terms, grad_w_conv, vector_terms))

    grad_list = []
    piece_lists = []
    collected = None
    for micro_index in range(step_count):
        grad_tokens, mol_pieces, local_grads = micro_step(micro_index * micro_rows)
        grad_list.append(grad_tokens)
        piece_lists.append(mol_pieces)
        collected = (
            local_grads if collected is None else jax.tree.map(jnp.add, collected, local_grads)
        )
    head_terms, conv_term, vector_terms = collected
    joined = head_terms[0]
    summed_heads = (
        lax.psum_scatter(
            joined[:, :local_width], ("pipe", "dp", "seq"), scatter_dimension=0, tiled=True
        ),
        lax.psum_scatter(
            joined[:, local_width : 2 * local_width],
            ("pipe", "dp", "seq"),
            scatter_dimension=0,
            tiled=True,
        ),
        lax.psum_scatter(
            joined[:, 2 * local_width :], ("pipe", "dp", "seq"), scatter_dimension=0, tiled=True
        ),
        lax.psum_scatter(head_terms[1], ("pipe", "dp", "seq"), scatter_dimension=1, tiled=True),
        lax.psum_scatter(head_terms[2], ("pipe", "dp", "seq"), scatter_dimension=0, tiled=True),
        lax.psum_scatter(head_terms[3], ("pipe", "dp", "seq"), scatter_dimension=1, tiled=True),
    )
    summed_conv = lax.psum_scatter(
        conv_term, ("pipe", "dp", "seq", "mp"), scatter_dimension=0, tiled=True
    )
    widened = tuple(
        (
            widen(item) if position in (0, 1, 5) else item
            for position, item in enumerate(vector_terms)
        )
    )
    summed_vectors = lax.psum(widened, ("pipe", "dp", "seq", "mp"))
    collected = (summed_heads, summed_conv, summed_vectors)
    input_grad = jnp.concatenate(grad_list, axis=0)
    moved = passed_along(input_grad[:, :, half_width:].astype(jnp.bfloat16), "pipe", 1).astype(
        jnp.float32
    )
    chars_grad = jnp.where(leading, input_grad[:, :, :half_width], moved)
    lower_all = jnp.concatenate([pieces[0] for pieces in piece_lists], axis=0)
    upper_all = jnp.concatenate([pieces[1] for pieces in piece_lists], axis=0)
    molecules = jnp.where(leading, lower_all, upper_all)
    summed_heads, summed_conv, summed_vectors = collected
    return (
        molecules,
        chars_grad,
        summed_heads[0],
        summed_vectors[0],
        summed_heads[1],
        summed_heads[2],
        summed_vectors[1],
        summed_heads[3],
        summed_vectors[2],
        summed_vectors[3],
        summed_vectors[4],
        summed_heads[4],
        summed_vectors[5],
        summed_heads[5],
        summed_vectors[6],
        summed_vectors[7],
        summed_vectors[8],
        summed_conv,
        summed_vectors[9],
        summed_vectors[10],
        summed_vectors[11],
    )


def solution(mesh):
    return jax.shard_map(
        on_device,
        mesh=mesh,
        in_specs=(
            P("dp", ("seq", "mp"), "pipe"),
            P("dp"),
            P(None, "mp"),
            P("mp"),
            P(None, "mp"),
            P(None, "mp"),
            P("mp"),
            P("mp", None),
            P(),
            P(),
            P(),
            P(None, "mp"),
            P("mp"),
            P("mp", None),
            P(),
            P(),
            P(),
            P(),
            P(),
            P(),
            P(),
            P("dp", ("seq", "mp"), "pipe"),
        ),
        out_specs=(
            P("dp", ("seq", "mp"), "pipe"),
            P("dp", ("seq", "mp"), "pipe"),
            P(("pipe", "dp", "seq"), "mp"),
            P(),
            P(("pipe", "dp", "seq"), "mp"),
            P(("pipe", "dp", "seq"), "mp"),
            P(),
            P("mp", ("pipe", "dp", "seq")),
            P(),
            P(),
            P(),
            P(("pipe", "dp", "seq"), "mp"),
            P(),
            P("mp", ("pipe", "dp", "seq")),
            P(),
            P(),
            P(),
            P(("pipe", "dp", "seq", "mp"), None),
            P(),
            P(),
            P(),
        ),
        check_vma=False,
    )
```

profile of v0, /device:TPU:0, one launch (start us, length us, event | category | flops | bytes accessed | tf_op | source)
XLA Modules:
  0.0 2110.8 jit_solution(2740783574834668998)
XLA Ops:
  21.6 23.4 %all-gather.17.cloned.1.call-done = bf16[1,1024,768]{2,1,0:T(8,128)(2,1)} async-done(((bf16[1,512,768]{2,1,0:T(8,128)(2,1)}), bf16[1,1024,768]{2,1,0:T(8,128)(2,1)}) %all-gather.17.cloned.1.call-update) | async-done | bytes 1572880 | tf_op jit(solution)/shard_map/all_gather | solution.py:58
  65.9 22.9 %conditional.45 = (bf16[1,1024,384]{1,2,0:T(8,128)(2,1)}, f32[1,8,6,128,1]{3,2,1,4,0:T(8,128)}, bf16[1,1024,768]{2,1,0:T(8,128)(2,1)S(1)}) conditional(s32[]{:T(128)} %convert_element_type.930, () %tuple.355, (bf16[2,1,1280,384]{2,3,1,0:T(8,128)(2,1)}, pred[1,8,128,384]{2,3,1,0:T(8,128)(4,1)}, bf16[1,1024,384]{1,2,0:T(8,128)(2,1)}, ...), branch_computations={%region_2.3_spmd, %region_3.6_spmd} | conditional | flops 1250813952 | bytes 150110464 | solution.py:50
  112.4 22.7 %conditional.51 = (bf16[1,1024,384]{1,2,0:T(8,128)(2,1)}, f32[1,8,6,128,1]{3,2,1,4,0:T(8,128)}, bf16[1,1024,768]{2,1,0:T(8,128)(2,1)S(1)}) conditional(s32[]{:T(128)} %convert_element_type.930, () %tuple.367, (bf16[2,1,1280,384]{2,3,1,0:T(8,128)(2,1)}, pred[1,8,128,384]{2,3,1,0:T(8,128)(4,1)}, bf16[1,1024,384]{1,2,0:T(8,128)(2,1)}, ...), branch_computations={%region_29.30_spmd, %region_30.0_spmd} | conditional | flops 1250813952 | bytes 150110464 | solution.py:50
  155.6 23.0 %conditional.57 = (bf16[1,1024,384]{1,2,0:T(8,128)(2,1)}, f32[1,8,6,128,1]{3,2,1,4,0:T(8,128)}, bf16[1,1024,768]{2,1,0:T(8,128)(2,1)S(1)}) conditional(s32[]{:T(128)} %convert_element_type.930, () %tuple.379, (bf16[2,1,1280,384]{2,3,1,0:T(8,128)(2,1)}, pred[1,8,128,384]{2,3,1,0:T(8,128)(4,1)}, bf16[1,1024,384]{1,2,0:T(8,128)(2,1)}, ...), branch_computations={%region_56.57_spmd, %region_57.0_spmd} | conditional | flops 1250813952 | bytes 150110464 | solution.py:50
  199.4 26.0 %conditional.63 = (bf16[1,1024,384]{1,2,0:T(8,128)(2,1)}, f32[1,8,6,128,1]{3,2,1,4,0:T(8,128)S(1)}, bf16[1,1024,768]{2,1,0:T(8,128)(2,1)}) conditional(s32[]{:T(128)} %convert_element_type.930, () %tuple.391, (bf16[2,1,1280,384]{2,3,1,0:T(8,128)(2,1)}, pred[1,8,128,384]{2,3,1,0:T(8,128)(4,1)}, bf16[1,1024,384]{1,2,0:T(8,128)(2,1)}, ...), branch_computations={%region_83.84_spmd, %region_84.87_spmd} | conditional | flops 1250813952 | bytes 149815456 | solution.py:50
  259.3 20.4 all-gather.19.cloned.1.call-done
  279.6 24.3 %conditional.47 = (f32[1,1024,1536]{2,1,0:T(8,128)}, bf16[1,1024,768]{2,1,0:T(8,128)(2,1)S(1)}) conditional(s32[]{:T(128)} %convert_element_type.930, () %tuple.360, (bf16[1,1024,768]{2,1,0:T(8,128)(2,1)}, bf16[768,1536]{1,0:T(8,128)(2,1)}, bf16[1536]{0:T(1024)(128)(2,1)S(1)}, bf16[1536,768]{1,0:T(8,128)(2,1)}) %tuple.868), branch_computations={%region_11.12_spmd, %region_12.13_spmd} | conditional | flops 4937221632 | bytes 42488876 | solution.py:50
  287.7 16.2 fusion.35
  308.3 24.5 %conditional.53 = (f32[1,1024,1536]{2,1,0:T(8,128)}, bf16[1,1024,768]{2,1,0:T(8,128)(2,1)S(1)}) conditional(s32[]{:T(128)} %convert_element_type.930, () %tuple.372, (bf16[1,1024,768]{2,1,0:T(8,128)(2,1)}, bf16[768,1536]{1,0:T(8,128)(2,1)}, bf16[1536]{0:T(1024)(128)(2,1)S(1)}, bf16[1536,768]{1,0:T(8,128)(2,1)}) %tuple.869), branch_computations={%region_38.39_spmd, %region_39.40_spmd} | conditional | flops 4937221632 | bytes 42488876 | solution.py:50
  316.6 16.2 fusion.124
  337.1 24.4 %conditional.59 = (f32[1,1024,1536]{2,1,0:T(8,128)}, bf16[1,1024,768]{2,1,0:T(8,128)(2,1)S(1)}) conditional(s32[]{:T(128)} %convert_element_type.930, () %tuple.384, (bf16[1,1024,768]{2,1,0:T(8,128)(2,1)}, bf16[768,1536]{1,0:T(8,128)(2,1)}, bf16[1536]{0:T(1024)(128)(2,1)S(1)}, bf16[1536,768]{1,0:T(8,128)(2,1)}) %tuple.870), branch_computations={%region_65.66_spmd, %region_66.67_spmd} | conditional | flops 4937221632 | bytes 42488876 | solution.py:50
  365.7 24.8 %conditional.65 = (f32[1,1024,1536]{2,1,0:T(8,128)}, bf16[1,1024,768]{2,1,0:T(8,128)(2,1)S(1)}) conditional(s32[]{:T(128)} %convert_element_type.930, () %tuple.396, (bf16[1,1024,768]{2,1,0:T(8,128)(2,1)}, bf16[768,1536]{1,0:T(8,128)(2,1)}, bf16[1536]{0:T(1024)(128)(2,1)S(1)}, bf16[1536,768]{1,0:T(8,128)(2,1)}) %tuple.871), branch_computations={%region_92.93_spmd, %region_93.94_spmd} | conditional | flops 4937221632 | bytes 42488876 | solution.py:50
  403.4 19.0 reduce-scatter.30.cloned.1.call-done
  476.4 21.3 %collective-permute-done.24 = bf16[1,512,768]{2,1,0:T(8,128)(2,1)S(1)} collective-permute-done((bf16[1,512,768]{2,1,0:T(8,128)(2,1)}, bf16[1,512,768]{2,1,0:T(8,128)(2,1)S(1)}, u32[]{:S(2)}, u32[]{:S(2)}) %collective-permute-start.24) | collective-permute-done | bytes 786464 | tf_op jit(solution)/shard_map/ppermute | solution.py:19
  549.5 18.4 collective-permute-done.27
  575.7 20.3 collective-permute-done.30
  606.6 49.4 %conditional.69 = (f32[1536]{0:T(1024)S(1)}, bf16[1,1024,768]{2,1,0:T(8,128)(2,1)}, f32[768,1536]{1,0:T(8,128)}, f32[1536,768]{0,1:T(8,128)}) conditional(s32[]{:T(128)} %convert_element_type.930, () %tuple.405, (f32[1,1024,1536]{2,1,0:T(8,128)}, bf16[1,1024,768]{2,1,0:T(8,128)(2,1)}, bf16[1536,768]{1,0:T(8,128)(2,1)}, ...), branch_computations={%region_116.117_spmd, %region_117.119_spmd} | conditional | flops 9791076352 | bytes 162011392 | solution.py:50
  656.6 49.3 %conditional.74 = (f32[1536]{0:T(1024)S(1)}, bf16[1,1024,768]{2,1,0:T(8,128)(2,1)}, f32[768,1536]{1,0:T(8,128)}, f32[1536,768]{0,1:T(8,128)}) conditional(s32[]{:T(128)} %convert_element_type.930, () %tuple.415, (f32[1,1024,1536]{2,1,0:T(8,128)}, bf16[1,1024,768]{2,1,0:T(8,128)(2,1)}, bf16[1536,768]{1,0:T(8,128)(2,1)}, ...), branch_computations={%region_143.144_spmd, %region_144.146_spmd} | conditional | flops 9791076352 | bytes 162011392 | solution.py:50
  706.6 49.0 %conditional.79 = (f32[1536]{0:T(1024)S(1)}, bf16[1,1024,768]{2,1,0:T(8,128)(2,1)}, f32[768,1536]{1,0:T(8,128)}, f32[1536,768]{0,1:T(8,128)}) conditional(s32[]{:T(128)} %convert_element_type.930, () %tuple.425, (f32[1,1024,1536]{2,1,0:T(8,128)}, bf16[1,1024,768]{2,1,0:T(8,128)(2,1)}, bf16[1536,768]{1,0:T(8,128)(2,1)}, ...), branch_computations={%region_170.171_spmd, %region_171.173_spmd} | conditional | flops 9791076352 | bytes 162011392 | solution.py:50
  756.2 49.2 %conditional.84 = (f32[1536]{0:T(1024)S(1)}, bf16[1,1024,768]{2,1,0:T(8,128)(2,1)}, f32[768,1536]{1,0:T(8,128)}, f32[1536,768]{0,1:T(8,128)}) conditional(s32[]{:T(128)} %convert_element_type.930, () %tuple.435, (f32[1,1024,1536]{2,1,0:T(8,128)}, bf16[1,1024,768]{2,1,0:T(8,128)(2,1)}, bf16[1536,768]{1,0:T(8,128)(2,1)}, ...), branch_computations={%region_197.198_spmd, %region_198.200_spmd} | conditional | flops 9791076352 | bytes 162011392 | solution.py:50
  860.8 131.2 %conditional.71 = (f32[1,1024,384]{1,0,2:T(1,128)}, f32[2,1,1280,384]{3,2,0,1:T(8,128)}, bf16[2,1,256,384]{3,2,0,1:T(8,128)(2,1)}, f32[384,768]{0,1:T(8,128)}) conditional(s32[]{:T(128)} %convert_element_type.930, () %tuple.401, (bf16[1,1024,384]{1,2,0:T(8,128)(2,1)}, bf16[1,1024,768]{2,1,0:T(8,128)(2,1)}, ...), branch_computations={%region_128.129_spmd, %region_129.131_spmd} | conditional | flops 2805216000 | bytes 242884928 | solution.py:50
  883.0 19.1 multiply_bitcast_fusion
  939.5 16.3 fusion.874
  966.0 18.4 multiply_bitcast_fusion.1
  1005.1 21.9 %conditional.72 = (f32[1152]{0:T(1024)S(1)}, bf16[1,1024,768]{2,1,0:T(8,128)(2,1)}, f32[768,1152]{1,0:T(8,128)S(1)}) conditional(s32[]{:T(128)} %convert_element_type.930, () %tuple.400, (f32[1,1024,384]{1,0,2:T(1,128)}, f32[2,1,1280,384]{3,2,0,1:T(8,128)}, f32[2,1,512,384]{3,2,1,0:T(8,128)S(1)}, bf16[1,1024,768]{2,1,0:T(8,128)(2,1)}, ...), branch_computations={%region_131.132_spmd, %region_132.134_spmd} | conditional | flops 3648650240 | bytes 54072000 | solution.py:50
  1028.8 134.1 %conditional.76 = (f32[1,1024,384]{1,0,2:T(1,128)}, f32[2,1,1280,384]{3,2,0,1:T(8,128)}, bf16[2,1,256,384]{3,2,0,1:T(8,128)(2,1)}, f32[384,768]{0,1:T(8,128)}) conditional(s32[]{:T(128)} %convert_element_type.930, () %tuple.411, (bf16[1,1024,384]{1,2,0:T(8,128)(2,1)}, bf16[1,1024,768]{2,1,0:T(8,128)(2,1)}, ...), branch_computations={%region_155.156_spmd, %region_156.158_spmd} | conditional | flops 2805216000 | bytes 246817088 | solution.py:50
  1054.0 19.1 multiply_bitcast_fusion.2
  1110.4 16.3 fusion.880
  1136.9 18.4 multiply_bitcast_fusion.3
  1173.9 21.7 %conditional.77 = (f32[1152]{0:T(1024)S(1)}, bf16[1,1024,768]{2,1,0:T(8,128)(2,1)}, f32[768,1152]{1,0:T(8,128)S(1)}) conditional(s32[]{:T(128)} %convert_element_type.930, () %tuple.410, (f32[1,1024,384]{1,0,2:T(1,128)}, f32[2,1,1280,384]{3,2,0,1:T(8,128)}, f32[2,1,512,384]{3,2,1,0:T(8,128)S(1)}, bf16[1,1024,768]{2,1,0:T(8,128)(2,1)}, ...), branch_computations={%region_158.159_spmd, %region_159.161_spmd} | conditional | flops 3648650240 | bytes 54072000 | solution.py:50
  1197.4 134.2 %conditional.81 = (f32[1,1024,384]{1,0,2:T(1,128)}, f32[2,1,1280,384]{3,2,0,1:T(8,128)}, bf16[2,1,256,384]{3,2,0,1:T(8,128)(2,1)}, f32[384,768]{0,1:T(8,128)}) conditional(s32[]{:T(128)} %convert_element_type.930, () %tuple.421, (bf16[1,1024,384]{1,2,0:T(8,128)(2,1)}, bf16[1,1024,768]{2,1,0:T(8,128)(2,1)}, ...), branch_computations={%region_182.183_spmd, %region_183.185_spmd} | conditional | flops 2805216000 | bytes 246817088 | solution.py:50
  1222.7 19.1 multiply_bitcast_fusion.4
  1279.1 16.3 fusion.886
  1305.6 18.5 multiply_bitcast_fusion.5
  1342.7 21.8 %conditional.82 = (f32[1152]{0:T(1024)S(1)}, bf16[1,1024,768]{2,1,0:T(8,128)(2,1)}, f32[768,1152]{1,0:T(8,128)S(1)}) conditional(s32[]{:T(128)} %convert_element_type.930, () %tuple.420, (f32[1,1024,384]{1,0,2:T(1,128)}, f32[2,1,1280,384]{3,2,0,1:T(8,128)}, f32[2,1,512,384]{3,2,1,0:T(8,128)S(1)}, bf16[1,1024,768]{2,1,0:T(8,128)(2,1)}, ...), branch_computations={%region_185.186_spmd, %region_186.188_spmd} | conditional | flops 3648650240 | bytes 54072000 | solution.py:50
  1366.2 134.1 %conditional.86 = (f32[1,1024,384]{1,0,2:T(1,128)}, f32[2,1,1280,384]{3,2,0,1:T(8,128)}, bf16[2,1,256,384]{3,2,0,1:T(8,128)(2,1)}, f32[384,768]{0,1:T(8,128)}) conditional(s32[]{:T(128)} %convert_element_type.930, () %tuple.431, (bf16[1,1024,384]{1,2,0:T(8,128)(2,1)}, bf16[1,1024,768]{2,1,0:T(8,128)(2,1)}, ...), branch_computations={%region_209.210_spmd, %region_210.212_spmd} | conditional | flops 2805216000 | bytes 246915424 | solution.py:50
  1391.5 19.1 multiply_bitcast_fusion.6
  1447.9 16.3 fusion.892
  1474.3 18.4 multiply_bitcast_fusion.7
  1511.4 21.4 %conditional.87 = (f32[1152]{0:T(1024)S(1)}, bf16[1,1024,768]{2,1,0:T(8,128)(2,1)}, f32[768,1152]{1,0:T(8,128)}) conditional(s32[]{:T(128)} %convert_element_type.930, () %tuple.430, (f32[1,1024,384]{1,0,2:T(1,128)}, f32[2,1,1280,384]{3,2,0,1:T(8,128)}, f32[2,1,512,384]{3,2,1,0:T(8,128)S(1)}, bf16[1,1024,768]{2,1,0:T(8,128)(2,1)}, ...), branch_computations={%region_212.213_spmd, %region_213.215_spmd} | conditional | flops 3648650240 | bytes 44634732 | solution.py:50
  1567.6 17.3 add_add_fusion.20
  1614.6 41.3 %all-reduce.20 = (f32[768]{0:T(1024)}, f32[768]{0:T(1024)}, f32[768]{0:T(1024)}, f32[768]{0:T(1024)}, f32[768]{0:T(1024)}, /*index=5*/f32[3072]{0:T(1024)}, f32[...) all-reduce(f32[768]{0:T(1024)S(1)} %add_dynamic-update-slice_fusion, ...), channel_id=1, replica_groups=mesh['pipe'=2,'dp'=4,'seq'=2,'mp'=2] {'pipe','dp','seq','mp'}, use_global_device_ids=true, to_apply=%region_217.218 | all-reduce | flops 11520 | bytes 92160 | tf_op jit(solution)/shard_map/psum | solution.py:435
  1659.7 22.1 %reduce-scatter.56.cloned.1.call-done = f32[48,384]{1,0:T(8,128)} async-done(((f32[768,384]{1,0:T(8,128)}), f32[48,384]{1,0:T(8,128)}) %reduce-scatter.56.cloned.1.call-update) | async-done | bytes 73744 | tf_op jit(solution)/shard_map/reduce_scatter | solution.py:410
  1681.8 61.2 %reduce-scatter.58.cloned.1.call-done = f32[48,384]{1,0:T(8,128)} async-done(((f32[768,384]{1,0:T(8,128)}), f32[48,384]{1,0:T(8,128)}) %reduce-scatter.58.cloned.1.call-update) | async-done | bytes 73744 | tf_op jit(solution)/shard_map/reduce_scatter | solution.py:413
  1743.0 61.2 %reduce-scatter.60.cloned.1.call-done = f32[48,384]{1,0:T(8,128)} async-done(((f32[768,384]{1,0:T(8,128)}), f32[48,384]{1,0:T(8,128)}) %reduce-scatter.60.cloned.1.call-update) | async-done | bytes 73744 | tf_op jit(solution)/shard_map/reduce_scatter | solution.py:419
  1804.2 78.9 %reduce-scatter.66.cloned.1.call-done = f32[1536,48]{0,1:T(8,128)} async-done(((f32[1536,768]{0,1:T(8,128)}), f32[1536,48]{0,1:T(8,128)}) %reduce-scatter.66.cloned.1.call-update) | async-done | bytes 294928 | tf_op jit(solution)/shard_map/reduce_scatter | solution.py:424
  1883.1 79.6 %reduce-scatter.64.cloned.1.call-done = f32[48,1536]{1,0:T(8,128)} async-done(((f32[768,1536]{1,0:T(8,128)}), f32[48,1536]{1,0:T(8,128)}) %reduce-scatter.64.cloned.1.call-update) | async-done | bytes 294928 | tf_op jit(solution)/shard_map/reduce_scatter | solution.py:423
  1962.7 141.1 %reduce-scatter.68.cloned.1.call-done = f32[96,768]{1,0:T(8,128)} async-done(((f32[3072,768]{1,0:T(8,128)}), f32[96,768]{1,0:T(8,128)}) %reduce-scatter.68.cloned.1.call-update) | async-done | bytes 294928 | tf_op jit(solution)/shard_map/reduce_scatter | solution.py:426
  (1193 shorter events, 1365.7 us)
Async XLA Ops:
  7.2 37.8 %all-gather.17.cloned.1.call-start = ((), (), s32[]{:S(2)}) async-start(), calls=%async_computation.23 | async-start | bytes 2359296 | tf_op jit(solution)/shard_map/all_gather | solution.py:58
  14.9 75.3 %all-gather.21.cloned.1.call-start = ((), (), s32[]{:S(2)}) async-start(), calls=%async_computation.27 | async-start | bytes 2359296 | tf_op jit(solution)/shard_map/all_gather | solution.py:58
  15.7 120.7 %all-gather.25.cloned.1.call-start = ((), (), s32[]{:S(2)}) async-start(), calls=%async_computation.31 | async-start | bytes 2359296 | tf_op jit(solution)/shard_map/all_gather | solution.py:58
  16.4 163.5 %all-gather.29.cloned.1.call-start = ((), (), s32[]{:S(2)}) async-start(), calls=%async_computation.35 | async-start | bytes 2359296 | tf_op jit(solution)/shard_map/all_gather | solution.py:58
  18.8 206.9 %reduce-scatter.24.cloned.1.call-start = ((), (), s32[]{:S(2)}) async-start(), calls=%async_computation.24 | async-start | bytes 2359296 | tf_op jit(solution)/shard_map/reduce_scatter | solution.py:62
  90.1 143.4 %reduce-scatter.28.cloned.1.call-start = ((), (), s32[]{:S(2)}) async-start(), calls=%async_computation.28 | async-start | bytes 2359296 | tf_op jit(solution)/shard_map/reduce_scatter | solution.py:62
  136.3 105.7 %reduce-scatter.32.cloned.1.call-start = ((), (), s32[]{:S(2)}) async-start(), calls=%async_computation.32 | async-start | bytes 2359296 | tf_op jit(solution)/shard_map/reduce_scatter | solution.py:62
  179.8 71.0 %reduce-scatter.36.cloned.1.call-start = ((), (), s32[]{:S(2)}) async-start(), calls=%async_computation.36 | async-start | bytes 2359296 | tf_op jit(solution)/shard_map/reduce_scatter | solution.py:62
  225.5 54.1 %all-gather.19.cloned.1.call-start = ((), (), s32[]{:S(2)}) async-start(), calls=%async_computation.25 | async-start | bytes 2359296 | tf_op jit(solution)/shard_map/all_gather | solution.py:58
  233.4 74.8 %all-gather.23.cloned.1.call-start = ((), (), s32[]{:S(2)}) async-start(), calls=%async_computation.29 | async-start | bytes 2359296 | tf_op jit(solution)/shard_map/all_gather | solution.py:58
  241.9 95.1 %all-gather.27.cloned.1.call-start = ((), (), s32[]{:S(2)}) async-start(), calls=%async_computation.33 | async-start | bytes 2359296 | tf_op jit(solution)/shard_map/all_gather | solution.py:58
  250.4 115.3 %all-gather.31.cloned.1.call-start = ((), (), s32[]{:S(2)}) async-start(), calls=%async_computation.37 | async-start | bytes 2359296 | tf_op jit(solution)/shard_map/all_gather | solution.py:58
  259.2 134.8 %reduce-scatter.26.cloned.1.call-start = ((), (), s32[]{:S(2)}) async-start(), calls=%async_computation.26 | async-start | bytes 2359296 | tf_op jit(solution)/shard_map/reduce_scatter | solution.py:62
  305.2 117.2 %reduce-scatter.30.cloned.1.call-start = ((), (), s32[]{:S(2)}) async-start(), calls=%async_computation.30 | async-start | bytes 2359296 | tf_op jit(solution)/shard_map/reduce_scatter | solution.py:62
  333.9 179.4 %reduce-scatter.34.cloned.1.call-start = ((), (), s32[]{:S(2)}) async-start(), calls=%async_computation.34 | async-start | bytes 2359296 | tf_op jit(solution)/shard_map/reduce_scatter | solution.py:62
  362.7 160.4 %reduce-scatter.38.cloned.1.call-start = ((), (), s32[]{:S(2)}) async-start(), calls=%async_computation.38 | async-start | bytes 2359296 | tf_op jit(solution)/shard_map/reduce_scatter | solution.py:62
  391.7 214.9 %all-gather.33.cloned.1.call-start = ((), (), s32[]{:S(2)}) async-start(), calls=%async_computation.39 | async-start | bytes 2359296 | tf_op jit(solution)/shard_map/all_gather | solution.py:58
  401.2 35.9 %collective-permute-start.3 = (bf16[1,512,768]{2,1,0:T(8,128)(2,1)}, bf16[1,512,768]{2,1,0:T(8,128)(2,1)}, u32[]{:S(2)}, u32[]{:S(2)}) collective-permute-start(bf16[1,512,768]{2,1,0:T(8,128)(2,1)} %get-tuple-element.812), channel_id=1, source_target_pairs={{0,16},{1,17},{2,18},{3,19},{4,20},{5,21},{6,22},{7,23},{8,24},{9,... | collective-permute-start | bytes 2359304 | tf_op jit(solution)/shard_map/ppermute | solution.py:19
  429.4 15.1 collective-permute-start.8
  443.2 25.3 %collective-permute-start.21 = (bf16[1,512,768]{2,1,0:T(8,128)(2,1)}, bf16[1,512,768]{2,1,0:T(8,128)(2,1)S(1)}, u32[]{:S(2)}, u32[]{:S(2)}) collective-permute-start(bf16[1,512,768]{2,1,0:T(8,128)(2,1)} %get-tuple-element.830), channel_id=1, source_target_pairs={{16,0},{17,1},{18,2},{19,3},{20,4},{21,5},{22,6},{23,7},{24,8},{25... | collective-permute-start | bytes 2359304 | tf_op jit(solution)/shard_map/ppermute | solution.py:19
  451.7 46.0 %collective-permute-start.24 = (bf16[1,512,768]{2,1,0:T(8,128)(2,1)}, bf16[1,512,768]{2,1,0:T(8,128)(2,1)S(1)}, u32[]{:S(2)}, u32[]{:S(2)}) collective-permute-start(bf16[1,512,768]{2,1,0:T(8,128)(2,1)} %get-tuple-element.843), channel_id=1, source_target_pairs={{16,0},{17,1},{18,2},{19,3},{20,4},{21,5},{22,6},{23,7},{24,8},{25... | collective-permute-start | bytes 2359304 | tf_op jit(solution)/shard_map/ppermute | solution.py:19
  511.4 144.7 %all-gather.37.cloned.1.call-start = ((), (), s32[]{:S(2)}) async-start(), calls=%async_computation.43 | async-start | bytes 2359296 | tf_op jit(solution)/shard_map/all_gather | solution.py:58
  520.6 15.0 collective-permute-start.13
  530.2 12.6 collective-permute-start.18
  534.1 171.9 %all-gather.41.cloned.1.call-start = ((), (), s32[]{:S(2)}) async-start(), calls=%async_computation.47 | async-start | bytes 2359296 | tf_op jit(solution)/shard_map/all_gather | solution.py:58
  541.5 26.4 %collective-permute-start.27 = (bf16[1,512,768]{2,1,0:T(8,128)(2,1)}, bf16[1,512,768]{2,1,0:T(8,128)(2,1)S(1)}, u32[]{:S(2)}, u32[]{:S(2)}) collective-permute-start(bf16[1,512,768]{2,1,0:T(8,128)(2,1)} %get-tuple-element.856), channel_id=1, source_target_pairs={{16,0},{17,1},{18,2},{19,3},{20,4},{21,5},{22,6},{23,7},{24,8},{25... | collective-permute-start | bytes 2359304 | tf_op jit(solution)/shard_map/ppermute | solution.py:19
  548.2 47.8 %collective-permute-start.30 = (bf16[1,512,768]{2,1,0:T(8,128)(2,1)}, bf16[1,512,768]{2,1,0:T(8,128)(2,1)S(1)}, u32[]{:S(2)}, u32[]{:S(2)}) collective-permute-start(bf16[1,512,768]{2,1,0:T(8,128)(2,1)} %copy-done.116), channel_id=1, source_target_pairs={{16,0},{17,1},{18,2},{19,3},{20,4},{21,5},{22,6},{23,7},{24,8},{25... | collective-permute-start | bytes 2359304 | tf_op jit(solution)/shard_map/ppermute | solution.py:19
  606.0 149.7 %all-gather.45.cloned.1.call-start = ((), (), s32[]{:S(2)}) async-start(), calls=%async_computation.51 | async-start | bytes 2359296 | tf_op jit(solution)/shard_map/all_gather | solution.py:58
  606.5 199.4 %reduce-scatter.40.cloned.1.call-start = ((), (), s32[]{:S(2)}) async-start(), calls=%async_computation.40 | async-start | bytes 2359296 | tf_op jit(solution)/shard_map/reduce_scatter | solution.py:62
  656.1 160.9 %reduce-scatter.44.cloned.1.call-start = ((), (), s32[]{:S(2)}) async-start(), calls=%async_computation.44 | async-start | bytes 2359296 | tf_op jit(solution)/shard_map/reduce_scatter | solution.py:62
  706.0 123.7 %reduce-scatter.48.cloned.1.call-start = ((), (), s32[]{:S(2)}) async-start(), calls=%async_computation.48 | async-start | bytes 2359296 | tf_op jit(solution)/shard_map/reduce_scatter | solution.py:62
  755.6 86.4 %reduce-scatter.52.cloned.1.call-start = ((), (), s32[]{:S(2)}) async-start(), calls=%async_computation.52 | async-start | bytes 2359296 | tf_op jit(solution)/shard_map/reduce_scatter | solution.py:62
  805.4 55.4 %all-gather.35.cloned.1.call-start = ((), (), s32[]{:S(2)}) async-start(), calls=%async_computation.41 | async-start | bytes 2359296 | tf_op jit(solution)/shard_map/all_gather | solution.py:58
  816.9 210.2 %all-gather.39.cloned.1.call-start = ((), (), s32[]{:S(2)}) async-start(), calls=%async_computation.45 | async-start | bytes 2359296 | tf_op jit(solution)/shard_map/all_gather | solution.py:58
  829.6 366.1 %all-gather.43.cloned.1.call-start = ((), (), s32[]{:S(2)}) async-start(), calls=%async_computation.49 | async-start | bytes 2359296 | tf_op jit(solution)/shard_map/all_gather | solution.py:58
  842.0 522.5 %all-gather.47.cloned.1.call-start = ((), (), s32[]{:S(2)}) async-start(), calls=%async_computation.53 | async-start | bytes 2359296 | tf_op jit(solution)/shard_map/all_gather | solution.py:58
  854.3 742.4 %reduce-scatter.42.cloned.1.call-start = ((), (), s32[]{:S(2)}) async-start(), calls=%async_computation.42 | async-start | bytes 2359296 | tf_op jit(solution)/shard_map/reduce_scatter | solution.py:62
  1027.1 572.1 %reduce-scatter.46.cloned.1.call-start = ((), (), s32[]{:S(2)}) async-start(), calls=%async_computation.46 | async-start | bytes 2359296 | tf_op jit(solution)/shard_map/reduce_scatter | solution.py:62
  1195.7 406.1 %reduce-scatter.50.cloned.1.call-start = ((), (), s32[]{:S(2)}) async-start(), calls=%async_computation.50 | async-start | bytes 2359296 | tf_op jit(solution)/shard_map/reduce_scatter | solution.py:62
  1364.4 239.9 %reduce-scatter.54.cloned.1.call-start = ((), (), s32[]{:S(2)}) async-start(), calls=%async_computation.54 | async-start | bytes 2359296 | tf_op jit(solution)/shard_map/reduce_scatter | solution.py:62
  1532.9 126.9 %reduce-scatter.62.cloned.1.call-start = ((), (), s32[]{:S(2)}) async-start(), calls=%async_computation.58 | async-start | bytes 1253376 | tf_op jit(solution)/shard_map/reduce_scatter | solution.py:422
  1536.7 145.1 %reduce-scatter.56.cloned.1.call-start = ((), (), s32[]{:S(2)}) async-start(), calls=%async_computation.55 | async-start | bytes 1253376 | tf_op jit(solution)/shard_map/reduce_scatter | solution.py:410
  1543.9 199.1 %reduce-scatter.58.cloned.1.call-start = ((), (), s32[]{:S(2)}) async-start(), calls=%async_computation.56 | async-start | bytes 1253376 | tf_op jit(solution)/shard_map/reduce_scatter | solution.py:413
  1544.6 259.6 %reduce-scatter.60.cloned.1.call-start = ((), (), s32[]{:S(2)}) async-start(), calls=%async_computation.57 | async-start | bytes 1253376 | tf_op jit(solution)/shard_map/reduce_scatter | solution.py:419
  1545.2 337.9 %reduce-scatter.66.cloned.1.call-start = ((), (), s32[]{:S(2)}) async-start(), calls=%async_computation.60 | async-start | bytes 5013504 | tf_op jit(solution)/shard_map/reduce_scatter | solution.py:424
  1556.2 406.5 %reduce-scatter.64.cloned.1.call-start = ((), (), s32[]{:S(2)}) async-start(), calls=%async_computation.59 | async-start | bytes 5013504 | tf_op jit(solution)/shard_map/reduce_scatter | solution.py:423
  1567.4 536.4 %reduce-scatter.68.cloned.1.call-start = ((), (), s32[]{:S(2)}) async-start(), calls=%async_computation.61 | async-start | bytes 9732096 | tf_op jit(solution)/shard_map/reduce_scatter | solution.py:426
  1611.3 44.6 %collective-permute-start.33 = (bf16[4,512,384]{2,1,0:T(8,128)(2,1)S(1)}, bf16[4,512,384]{2,1,0:T(8,128)(2,1)S(1)}, u32[]{:S(2)}, u32[]{:S(2)}) collective-permute-start(bf16[4,512,384]{2,1,0:T(8,128)(2,1)S(1)} %slice.704), channel_id=1, source_target_pairs={{0,16},{1,17},{2,18},{3,19},{4,20},{5,21},{6,22},{7,23},{8,24},{9,... | collective-permute-start | bytes 4718600 | tf_op jit(solution)/shard_map/ppermute | solution.py:19
  (258 other events, 1954.3 us)
Sparse Core Ops, SparseCore 0:
  15.0 29.9 all-gather.16
  46.5 27.1 all-gather.20
  75.3 27.1 all-gather.24
  104.0 27.1 all-gather.28
  133.3 26.0 reduce-scatter.23
  161.6 26.0 reduce-scatter.27
  190.0 26.0 reduce-scatter.31
  225.6 25.1 reduce-scatter.35
  252.4 27.2 all-gather.18
  281.0 27.2 all-gather.22
  309.8 27.2 all-gather.26
  338.5 27.1 all-gather.30
  367.9 26.0 reduce-scatter.25
  396.3 26.0 reduce-scatter.29
  424.5 26.0 reduce-scatter.33
  452.8 26.0 reduce-scatter.37
  511.5 27.6 all-gather.32
  540.6 27.2 all-gather.36
  606.1 27.5 all-gather.40
  635.1 27.2 all-gather.44
  664.6 26.0 reduce-scatter.39
  706.1 26.4 reduce-scatter.43
  755.7 26.4 reduce-scatter.47
  805.5 26.4 reduce-scatter.51
  833.6 27.1 all-gather.34
  862.2 27.1 all-gather.38
  890.8 27.2 all-gather.42
  919.6 27.2 all-gather.46
  1027.2 25.2 reduce-scatter.41
  1195.8 25.2 reduce-scatter.45
  1364.6 25.2 reduce-scatter.49
  1533.0 25.2 reduce-scatter.53
  1562.3 57.9 reduce-scatter.61
  1624.5 57.2 reduce-scatter.55
  1686.0 56.9 reduce-scatter.57
  1747.0 57.1 reduce-scatter.59
  1808.5 74.6 reduce-scatter.65
  1888.1 74.6 reduce-scatter.63
  1969.1 134.6 reduce-scatter.67
where the time goes:
time: 2120 us; the launch traced here: 2110 us
  waiting for transfers between devices  646 us (30%)
  matrix products  528 us (25%)
  local copies, waits for them, and re-layouts  464 us (22%)
  other arithmetic  348 us (16%)
  starting transfers between devices  57.1 us (3%)
  blocking collectives  41.3 us (2%)
    reduce_scatter x1, waiting for transfers between devices, on_device(): lax.psum_scatter(conv_term, ('pipe', 'dp', 'seq', 'mp'), scatter_dimensio...  141 us
    dot_general x16, matrix products, apply_right(): jnp.einsum('bsi,ij->bsj', left, right, preferred_element_type=jnp.float32)  106 us
    another operation x12, local copies, waits for them, and re-layouts, attention_backward(): jnp.stack([grad_key_win, grad_value_win], axis=0)  91 us
    dot_general x16, matrix products, apply_transposed(): jnp.einsum('bsj,ij->bsi', left, right, preferred_element_type=jnp.float32)  87.6 us
    cond x308, local copies, waits for them, and re-layouts  80.3 us
    reduce_scatter x1, waiting for transfers between devices, on_device(): lax.psum_scatter(head_terms[2], ('pipe', 'dp', 'seq'), scatter_dimension=...  79.6 us
    reduce_scatter x1, waiting for transfers between devices, on_device(): lax.psum_scatter(head_terms[3], ('pipe', 'dp', 'seq'), scatter_dimension=...  78.9 us
    ppermute x18, waiting for transfers between devices, passed_along(): return lax.ppermute(block, axis, route)  78.5 us
  transfers between devices with their start and end apart: 73, of which 36 were waited for; matrix products, arithmetic and copies ran while one was open for 61% of the time, Pallas kernels for 0%

commit v1 on v0

v1 whole, which is shorter than its diff:
```python
import functools

import jax
import jax.numpy as jnp
from jax import lax
from jax.experimental import pallas as pl
from jax.experimental.pallas import tpu as pltpu
from jax.sharding import PartitionSpec as P

HEAD = 64
WINDOW = 128
KERNEL = 4
PAIR = 2 * HEAD
VMEM_LIMIT = 56 << 20

epsilon = 1e-05
masked_score = -1e30
f32 = jnp.float32
bf16 = jnp.bfloat16


def mul(left, right):
    return jnp.dot(left, right, preferred_element_type=f32)


def mul_t(left, right):
    return lax.dot_general(left, right, (((1,), (1,)), ((), ())), preferred_element_type=f32)


def t_mul(left, right):
    return lax.dot_general(left, right, (((0,), (0,)), ((), ())), preferred_element_type=f32)


def gelu_parts(value):
    bell = jnp.exp(value * value * -0.5)
    t = 1.0 / (1.0 + jnp.abs(value) * 0.23164190)
    poly = t * (0.127414796 + t * (-0.142248368 + t * (0.7107068705 + t * (-0.7265760135 + t * 0.5307027145))))
    tail = poly * bell
    cdf = jnp.where(value < 0.0, tail, 1.0 - tail)
    return value * cdf, cdf + value * bell * 0.3989422804014327


def norm_parts(value):
    centered = value - jnp.mean(value, axis=-1, keepdims=True)
    scale = lax.rsqrt(jnp.mean(centered * centered, axis=-1, keepdims=True) + epsilon)
    return centered * scale, scale


def norm_back(cotangent, normal, scale):
    first = jnp.mean(cotangent, axis=-1, keepdims=True)
    second = jnp.mean(cotangent * normal, axis=-1, keepdims=True)
    return scale * (cotangent - first - normal * second)


def col_sum(value):
    return jnp.sum(value, axis=0, keepdims=True)


def low(value):
    return value.astype(bf16)


def call(body, grid, in_specs, out_specs, out_shape, args, scalars=(), scratch=(), flops=0, moved=0):
    return pl.pallas_call(
        body,
        grid_spec=pltpu.PrefetchScalarGridSpec(
            num_scalar_prefetch=len(scalars),
            grid=grid,
            in_specs=in_specs,
            out_specs=out_specs,
            scratch_shapes=scratch,
        ),
        out_shape=out_shape,
        compiler_params=pltpu.CompilerParams(vmem_limit_bytes=VMEM_LIMIT),
        cost_estimate=pl.CostEstimate(flops=int(flops), bytes_accessed=int(moved), transcendentals=0),
    )(*scalars, *args)


def whole_block(array):
    zeros = (0,) * array.ndim
    return pl.BlockSpec(array.shape, lambda *_: zeros, pipeline_mode=pl.Buffered(1))


def lead_block(array, size=1):
    rest = (0,) * (array.ndim - 1)
    return pl.BlockSpec((size,) + tuple(array.shape[1:]), lambda i, *_: (i,) + rest)


def chunk_block(array, size):
    return pl.BlockSpec((array.shape[0], size, array.shape[2]), lambda i, *_: (0, i, 0))


def shape_of(dims, kind):
    return jax.ShapeDtypeStruct(tuple(dims), kind)


def pair_lanes(rows):
    return lax.broadcasted_iota(jnp.int32, (rows, PAIR), 1) < HEAD


def split_pair(both, is_first):
    zero = jnp.zeros_like(both)
    return jnp.concatenate([jnp.where(is_first, both, zero), jnp.where(is_first, zero, both)], axis=0)


def join_pair(stacked, is_first):
    rows = stacked.shape[0] // 2
    return jnp.where(is_first, stacked[:rows], stacked[rows:])


def attend_kernel(span, block, last, info_ref, x_ref, w_ref, bq_ref, bv_ref, *refs):
    if last:
        part_ref, bo_ref, gain_ref, shift_ref = refs[:4]
        refs = refs[4:]
    q_ref, k_ref, v_ref, att_ref, lse_ref = refs[:5]
    refs = refs[5:]
    row = pl.program_id(0)
    length = info_ref[row + 1]
    start = info_ref[0]
    width = block + 2 * WINDOW
    pairs = q_ref.shape[2] // PAIR
    x = x_ref[0]
    own = x_ref[0, WINDOW : WINDOW + span]
    q_ref[0] = low(low(mul(own, w_ref[0]) + bq_ref[...]).astype(f32) * HEAD ** (-0.5))
    k_ref[0] = low(mul(x, w_ref[1]))
    v_ref[0] = low(mul(x, w_ref[2]) + bv_ref[...])
    is_first = pair_lanes(block)
    q_at = lax.broadcasted_iota(jnp.int32, (block, width), 0)
    k_at = lax.broadcasted_iota(jnp.int32, (block, width), 1) - WINDOW
    in_window = jnp.abs(q_at - k_at) < WINDOW
    lanes = lax.broadcasted_iota(jnp.int32, (block, PAIR), 1)

    def one_block(index, carry):
        at = pl.multiple_of(index * block, block)
        position = k_at + (start + at)
        bias = jnp.where(in_window & (position >= 0) & (position < length), 0.0, masked_score)
        bias = jnp.concatenate([bias, bias], axis=0)
        totals = jnp.zeros((block, PAIR), f32)
        for pair in range(pairs):
            cols = slice(pair * PAIR, (pair + 1) * PAIR)
            q2 = split_pair(q_ref[0, pl.ds(at, block), cols], is_first)
            scores = mul_t(q2, k_ref[0, pl.ds(at, width), cols]) + bias
            top = jnp.max(scores, axis=-1, keepdims=True)
            weights = jnp.exp(scores - top)
            total = jnp.sum(weights, axis=-1, keepdims=True)
            out = mul(low(weights), v_ref[0, pl.ds(at, width), cols]) * (1.0 / total)
            att_ref[0, pl.ds(at, block), cols] = low(join_pair(out, is_first))
            log_total = top + jnp.log(total)
            totals = jnp.where(lanes == 2 * pair, log_total[:block], totals)
            totals = jnp.where(lanes == 2 * pair + 1, log_total[block:], totals)
        lse_ref[0, index] = totals.T[:8]
        return carry

    lax.fori_loop(0, span // block, one_block, 0)
    branch = mul_t(att_ref[0], w_ref[3])
    if last:
        n_ref, s_ref, mid_ref = refs
        before = own.astype(f32) + part_ref[0] + branch + bo_ref[...]
        normal, scale = norm_parts(before)
        n_ref[0] = normal
        s_ref[0] = jnp.broadcast_to(scale, s_ref.shape[1:])
        mid_ref[0] = low(normal * gain_ref[...] + shift_ref[...])
    else:
        refs[0][0] = branch


def attend(info, x_ext, w4, b_query, b_value, span, block, tail=None):
    rows, extent, model = x_ext.shape
    local = w4.shape[2]
    out_shape = [
        shape_of((rows, span, local), bf16),
        shape_of((rows, extent, local), bf16),
        shape_of((rows, extent, local), bf16),
        shape_of((rows, span, local), bf16),
        shape_of((rows, span // block, 8, block), f32),
    ]
    args = [x_ext, w4, b_query, b_value]
    in_specs = [lead_block(x_ext)] + [whole_block(a) for a in args[1:]]
    if tail is None:
        out_shape += [shape_of((rows, span, model), f32)]
    else:
        out_shape += [
            shape_of((rows, span, model), f32),
            shape_of((rows, span, PAIR), f32),
            shape_of((rows, span, model), bf16),
        ]
        args += list(tail)
        in_specs += [lead_block(tail[0])] + [whole_block(a) for a in tail[1:]]
    flops = 2 * rows * local * (model * (2 * span + 2 * extent) + span * 4 * (block + 2 * WINDOW))
    return call(
        functools.partial(attend_kernel, span, block, tail is not None),
        (rows,),
        in_specs,
        [lead_block(o) for o in out_shape],
        out_shape,
        args,
        scalars=(info,),
        flops=3 * flops,
        moved=rows * extent * model * 8,
    )


def attend_back_kernel(span, block, info_ref, gb_ref, w_ref, q_ref, k_ref, v_ref, lse_ref, dq_ref, dk_ref, dv_ref, ga_ref, dk_acc, dv_acc):
    row = pl.program_id(0)
    length = info_ref[row + 1]
    start = info_ref[0]
    width = block + 2 * WINDOW
    pairs = q_ref.shape[2] // PAIR
    ga_ref[...] = low(mul(gb_ref[0], w_ref[0]))
    dk_acc[...] = jnp.zeros_like(dk_acc)
    dv_acc[...] = jnp.zeros_like(dv_acc)
    is_first = pair_lanes(block)
    q_at = lax.broadcasted_iota(jnp.int32, (width, block), 1)
    k_at = lax.broadcasted_iota(jnp.int32, (width, block), 0) - WINDOW
    in_window = jnp.abs(q_at - k_at) < WINDOW

    def one_block(index, carry):
        at = pl.multiple_of(index * block, block)
        position = k_at + (start + at)
        bias = jnp.where(in_window & (position >= 0) & (position < length), 0.0, masked_score)
        bias = jnp.concatenate([bias, bias], axis=1)
        for pair in range(pairs):
            cols = slice(pair * PAIR, (pair + 1) * PAIR)
            keys = k_ref[0, pl.ds(at, width), cols]
            q2 = split_pair(q_ref[0, pl.ds(at, block), cols], is_first)
            g2 = split_pair(ga_ref[pl.ds(at, block), cols], is_first)
            log_total = jnp.concatenate(
                [lse_ref[0, index, 2 * pair : 2 * pair + 1], lse_ref[0, index, 2 * pair + 1 : 2 * pair + 2]], axis=1
            )
            probs = jnp.exp(mul_t(keys, q2) + bias - log_total)
            grad_probs = mul_t(v_ref[0, pl.ds(at, width), cols], g2)
            inner = jnp.sum(probs * grad_probs, axis=0, keepdims=True)
            grad_scores = low(probs * (grad_probs - inner))
            dk_acc[pl.ds(at, width), cols] += mul(grad_scores, q2)
            dv_acc[pl.ds(at, width), cols] += mul(low(probs), g2)
            grad_q = t_mul(grad_scores, keys) * HEAD ** (-0.5)
            dq_ref[0, pl.ds(at, block), cols] = low(join_pair(grad_q, is_first))
        return carry

    lax.fori_loop(0, span // block, one_block, 0)
    dk_ref[0] = low(dk_acc[...])
    dv_ref[0] = low(dv_acc[...])


def attend_back(info, grad_branch, w4, queries, keys, values, log_totals, block):
    rows, span, local = queries.shape
    extent = keys.shape[1]
    model = grad_branch.shape[2]
    out_shape = [
        shape_of((rows, span, local), bf16),
        shape_of((rows, extent, local), bf16),
        shape_of((rows, extent, local), bf16),
    ]
    args = [grad_branch, w4, queries, keys, values, log_totals]
    in_specs = [lead_block(a) for a in args]
    in_specs[1] = pl.BlockSpec((1,) + tuple(w4.shape[1:]), lambda i, *_: (3, 0, 0))
    return call(
        functools.partial(attend_back_kernel, span, block),
        (rows,),
        in_specs,
        [lead_block(o) for o in out_shape],
        out_shape,
        args,
        scalars=(info,),
        scratch=[pltpu.VMEM((span, local), bf16), pltpu.VMEM((extent, local), f32), pltpu.VMEM((extent, local), f32)],
        flops=6 * rows * span * local * (model + 5 * (block + 2 * WINDOW)),
        moved=rows * extent * model * 8,
    )


def feed_kernel(last, x_ref, wi_ref, wo_ref, bi_ref, *refs):
    if last:
        part_ref, n_ref, live_ref, g1_ref, s1_ref, bo_ref, g2_ref, s2_ref = refs[:8]
        refs = refs[8:]
    act_ref, slope_ref = refs[:2]
    x = x_ref[...]
    units = wi_ref.shape[1]
    step = 512
    total = None
    for at in range(0, units, step):
        cols = slice(at, at + step)
        act, slope = gelu_parts(mul(x, wi_ref[:, cols]) + bi_ref[:, cols])
        act = low(act)
        act_ref[:, cols] = act
        slope_ref[:, cols] = low(slope)
        term = mul(act, wo_ref[cols, :])
        total = term if total is None else total + term
    if last:
        n2_ref, scale_ref, sent_ref = refs[2:]
        middle = n_ref[...] * g1_ref[...] + s1_ref[...]
        normal, scale = norm_parts(middle + part_ref[...] + total + bo_ref[...])
        n2_ref[...] = normal
        scale_ref[...] = jnp.broadcast_to(scale, scale_ref.shape)
        sent = (normal * g2_ref[...] + s2_ref[...]) * live_ref[:, :1]
        for c in range(sent_ref.shape[0]):
            sent_ref[c] = sent[:, c * PAIR : (c + 1) * PAIR]
    else:
        refs[2][...] = total


def feed(middle, w_inner, w_outer, b_inner, tile, tail=None):
    tokens, model = middle.shape
    units = w_inner.shape[1]
    args = [middle, w_inner, w_outer, b_inner]
    in_specs = [lead_block(middle, tile)] + [whole_block(a) for a in args[1:]]
    out_shape = [shape_of((tokens, units), bf16), shape_of((tokens, units), bf16)]
    if tail is None:
        out_shape += [shape_of((tokens, model), f32)]
    else:
        out_shape += [shape_of((tokens, model), f32), shape_of((tokens, PAIR), f32)]
        args += list(tail)
        in_specs += [lead_block(a, tile) for a in tail[:3]] + [whole_block(a) for a in tail[3:]]
    out_specs = [lead_block(o, tile) for o in out_shape]
    if tail is not None:
        out_shape.append(shape_of((model // PAIR, tokens, PAIR), f32))
        out_specs.append(chunk_block(out_shape[-1], tile))
    return call(
        functools.partial(feed_kernel, tail is not None),
        (tokens // tile,),
        in_specs,
        out_specs,
        out_shape,
        args,
        flops=4 * tokens * model * units * 1.5,
        moved=tokens * units * 8,
    )


def conv_kernel(mols, sent_ref, wc_ref, bc_ref, g3_ref, s3_ref, g2_ref, mg_ref, ml_ref, n2_ref, sc_ref, lv_ref,
                mol_ref, gc_ref, grp_ref, two_ref, feed_ref, vec_ref, back_ref):
    @pl.when(pl.program_id(0) == 0)
    def _():
        vec_ref[...] = jnp.zeros_like(vec_ref)

    chunks = range(sent_ref.shape[0])
    total = None
    for k in range(KERNEL):
        grouped = low(jnp.concatenate([sent_ref[c, pl.ds(k, mols, stride=KERNEL), :] for c in chunks], axis=1))
        grp_ref[k] = grouped
        term = mul(grouped, wc_ref[k])
        total = term if total is None else total + term
    value, slope = gelu_parts(total + bc_ref[...])
    normal, scale = norm_parts(value)
    alive = ml_ref[:, :1]
    cotangent = mg_ref[...].astype(f32) * alive
    mol_ref[...] = low((normal * g3_ref[...] + s3_ref[...]) * alive)
    grad = low(norm_back(cotangent * g3_ref[...], normal, scale) * slope)
    gc_ref[...] = grad
    for k in range(KERNEL):
        back = low(mul_t(grad, wc_ref[k])).astype(f32)
        for c in chunks:
            back_ref[c, pl.ds(k, mols, stride=KERNEL), :] = back[:, c * PAIR : (c + 1) * PAIR]
    masked = jnp.concatenate([back_ref[c] for c in chunks], axis=1) * lv_ref[:, :1]
    n2 = n2_ref[...]
    grad_two = norm_back(masked * g2_ref[...], n2, sc_ref[:, :1])
    two_ref[...] = grad_two
    feed_ref[...] = low(grad_two)
    vec_ref[...] += jnp.concatenate(
        [
            col_sum(grad.astype(f32)),
            col_sum(cotangent * normal),
            col_sum(cotangent),
            col_sum(masked * n2),
            col_sum(masked),
            col_sum(grad_two),
            jnp.zeros((2, grad_two.shape[1]), f32),
        ],
        axis=0,
    )


def conv(sent, w_conv, b_conv, gain_three, shift_three, gain_two, mol_grad, live_mols, n2, scale2, live, steps):
    chunks, tokens, _ = sent.shape
    model = chunks * PAIR
    tile = tokens // steps
    mols = tile // KERNEL
    all_mols = tokens // KERNEL
    args = [sent, w_conv, b_conv, gain_three, shift_three, gain_two, mol_grad, live_mols, n2, scale2, live]
    in_specs = (
        [chunk_block(sent, tile)]
        + [whole_block(a) for a in args[1:6]]
        + [lead_block(a, mols) for a in args[6:8]]
        + [lead_block(a, tile) for a in args[8:]]
    )
    out_shape = [
        shape_of((all_mols, model), bf16),
        shape_of((all_mols, model), bf16),
        shape_of((KERNEL, all_mols, model), bf16),
        shape_of((tokens, model), f32),
        shape_of((tokens, model), bf16),
        shape_of((8, model), f32),
    ]
    out_specs = [
        lead_block(out_shape[0], mols),
        lead_block(out_shape[1], mols),
        pl.BlockSpec((KERNEL, mols, model), lambda i, *_: (0, i, 0)),
        lead_block(out_shape[3], tile),
        lead_block(out_shape[4], tile),
        pl.BlockSpec((8, model), lambda i, *_: (0, 0)),
    ]
    return call(
        functools.partial(conv_kernel, mols),
        (steps,),
        in_specs,
        out_specs,
        out_shape,
        args,
        scratch=[pltpu.VMEM((chunks, tile, PAIR), f32)],
        flops=4 * tokens * model * model * 1.5,
        moved=tokens * model * 30,
    )


def conv_weight_kernel(side_ref, grp_ref, grad_ref, *refs):
    value = t_mul(grp_ref[0], grad_ref[...])
    if len(refs) == 2:
        value = value + refs[0][0].astype(f32)
    refs[-1][0] = low(value)


def conv_weight(side, grouped, grad, got=None):
    kernel, mols, model = grouped.shape
    half = kernel // 2
    args = [grouped, grad]
    in_specs = [pl.BlockSpec((1, mols, model), lambda i, side_ref: (side_ref[0] * half + i, 0, 0)), whole_block(grad)]
    out_shape = shape_of((half, model, model), bf16)
    if got is not None:
        args.append(got)
        in_specs.append(lead_block(got))
    return call(
        conv_weight_kernel,
        (half,),
        in_specs,
        lead_block(out_shape),
        out_shape,
        args,
        scalars=(side,),
        flops=2 * half * mols * model * model,
        moved=half * model * model * 8,
    )


def weight_kernel(side_ref, left_ref, *refs):
    rights, refs = refs[:2], refs[2:]
    for index in range(2):
        value = t_mul(left_ref[...], rights[index][...])
        if len(refs) == 2:
            value = value + refs[0][index].astype(f32)
        refs[-1][index] = low(value)


def weight(side, left, right_own, right_other, got=None, tile=512):
    tokens, model = left.shape
    columns = right_own.shape[1]
    half = model // 2
    args = [left, right_own, right_other]
    in_specs = [
        pl.BlockSpec((tokens, half), lambda i, side_ref: (0, side_ref[0])),
        pl.BlockSpec((tokens, tile), lambda i, *_: (0, i)),
        pl.BlockSpec((tokens, tile), lambda i, *_: (0, i)),
    ]
    out_shape = shape_of((2, half, columns), bf16)
    out_spec = pl.BlockSpec((2, half, tile), lambda i, *_: (0, 0, i))
    if got is not None:
        args.append(got)
        in_specs.append(out_spec)
    return call(
        weight_kernel,
        (columns // tile,),
        in_specs,
        out_spec,
        out_shape,
        args,
        scalars=(side,),
        flops=4 * tokens * half * columns,
        moved=tokens * columns * 4 + half * columns * 8,
    )


def project_weight_kernel(span, side_ref, x_ref, gb_ref, *refs):
    groups, refs = refs[:8], refs[8:]
    which = pl.program_id(0)
    rows = x_ref.shape[0]
    for index in range(2):

        @pl.when(which == index)
        def _(index=index):
            dq, dk, dv, att = groups[4 * index : 4 * index + 4]
            local = dq.shape[2]
            for place, right in enumerate((dq, dk, dv, att)):
                value = None
                for row in range(rows):
                    if place == 0:
                        left = x_ref[row, WINDOW : WINDOW + span]
                    elif place == 3:
                        left = gb_ref[row]
                    else:
                        left = x_ref[row]
                    term = t_mul(left, right[row])
                    value = term if value is None else value + term
                cols = slice(place * local, (place + 1) * local)
                if len(refs) == 2:
                    value = value + refs[0][0, :, cols].astype(f32)
                refs[-1][0, :, cols] = low(value)


def project_weight(side, x_ext, grad_branch, own, other, span, got=None):
    rows, extent, model = x_ext.shape
    half = model // 2
    local = own[0].shape[2]
    args = [x_ext, grad_branch, *own, *other]
    in_specs = [
        pl.BlockSpec((rows, extent, half), lambda i, side_ref: (0, 0, side_ref[0])),
        pl.BlockSpec((rows, span, half), lambda i, side_ref: (0, 0, side_ref[0])),
    ] + [whole_block(a) for a in args[2:]]
    out_shape = shape_of((2, half, 4 * local), bf16)
    if got is not None:
        args.append(got)
        in_specs.append(lead_block(got))
    return call(
        functools.partial(project_weight_kernel, span),
        (2,),
        in_specs,
        lead_block(out_shape),
        out_shape,
        args,
        scalars=(side,),
        flops=16 * rows * extent * half * local,
        moved=rows * extent * model * 12,
    )


def feed_back_kernel(gf_ref, two_ref, sl_own, sl_other, n_ref, sc_ref, wo_own, wo_other, wi_own, wi_other, g1_ref,
                     gh_own, gh_other, one_ref, gb_ref, vec_ref, bi_own, bi_other):
    @pl.when(pl.program_id(0) == 0)
    def _():
        vec_ref[...] = jnp.zeros_like(vec_ref)
        bi_own[...] = jnp.zeros_like(bi_own)
        bi_other[...] = jnp.zeros_like(bi_other)

    grad_feed = gf_ref[...]
    units = wo_own.shape[0]
    step = 512
    total = two_ref[...]
    for slope_ref, wo_ref, wi_ref, gh_ref, bi_ref in (
        (sl_own, wo_own, wi_own, gh_own, bi_own),
        (sl_other, wo_other, wi_other, gh_other, bi_other),
    ):
        for at in range(0, units, step):
            cols = slice(at, at + step)
            grad = low(mul_t(grad_feed, wo_ref[cols, :]) * slope_ref[:, cols].astype(f32))
            gh_ref[:, cols] = grad
            bi_ref[:1, cols] += col_sum(grad.astype(f32))
            total = total + mul_t(grad, wi_ref[:, cols])
    normal = n_ref[...]
    grad_one = norm_back(total * g1_ref[...], normal, sc_ref[:, :1])
    one_ref[...] = grad_one
    gb_ref[...] = low(grad_one)
    vec_ref[...] += jnp.concatenate(
        [col_sum(grad_one), col_sum(total * normal), col_sum(total), jnp.zeros((5, total.shape[1]), f32)], axis=0
    )


def feed_back(grad_feed, grad_two, slopes, n1, scale1, outers, inners, gain_one, tile):
    tokens, model = grad_feed.shape
    units = outers[0].shape[0]
    args = [grad_feed, grad_two, *slopes, n1, scale1, *outers, *inners, gain_one]
    in_specs = [lead_block(a, tile) for a in args[:6]] + [whole_block(a) for a in args[6:]]
    out_shape = [
        shape_of((tokens, units), bf16),
        shape_of((tokens, units), bf16),
        shape_of((tokens, model), f32),
        shape_of((tokens, model), bf16),
        shape_of((8, model), f32),
        shape_of((8, units), f32),
        shape_of((8, units), f32),
    ]
    out_specs = [lead_block(o, tile) for o in out_shape[:4]] + [
        pl.BlockSpec(o.shape, lambda i, *_: (0, 0)) for o in out_shape[4:]
    ]
    return call(
        feed_back_kernel,
        (tokens // tile,),
        in_specs,
        out_specs,
        out_shape,
        args,
        flops=8 * tokens * model * units * 1.2,
        moved=tokens * units * 8,
    )


def input_back_kernel(span, one_ref, *refs):
    groups, (own_w, other_w), (mid_ref, left_ref, right_ref, vec_ref) = refs[:6], refs[6:8], refs[8:]

    @pl.when(pl.program_id(0) == 0)
    def _():
        vec_ref[...] = jnp.zeros_like(vec_ref)

    total = None
    center = one_ref[0]
    sums = []
    for (dq, dk, dv), w_ref in ((groups[:3], own_w), (groups[3:], other_w)):
        center = center + mul_t(dq[0], w_ref[0])
        term = mul_t(dk[0], w_ref[1]) + mul_t(dv[0], w_ref[2])
        total = term if total is None else total + term
        sums.append(jnp.concatenate([col_sum(dq[0].astype(f32)), col_sum(dv[0].astype(f32))], axis=0))
    mid_ref[0] = center + total[WINDOW : WINDOW + span]
    left_ref[0] = low(total[:WINDOW])
    right_ref[0] = low(total[WINDOW + span :])
    rest = jnp.zeros((4, sums[0].shape[1]), f32)
    vec_ref[...] += jnp.concatenate(sums + [rest], axis=0)


def input_back(grad_one, own, other, w_own, w_other, span):
    rows, extent, local = own[1].shape
    model = grad_one.shape[2]
    args = [grad_one, *own, *other, w_own, w_other]
    in_specs = [lead_block(a) for a in args[:7]] + [whole_block(a) for a in args[7:]]
    out_shape = [
        shape_of((rows, span, model), f32),
        shape_of((rows, WINDOW, model), bf16),
        shape_of((rows, WINDOW, model), bf16),
        shape_of((8, local), f32),
    ]
    out_specs = [lead_block(o) for o in out_shape[:3]] + [pl.BlockSpec(out_shape[3].shape, lambda i, *_: (0, 0))]
    return call(
        functools.partial(input_back_kernel, span),
        (rows,),
        in_specs,
        out_specs,
        out_shape,
        args,
        flops=12 * rows * extent * model * local,
        moved=rows * extent * model * 12,
    )


def swapped(block, axis, bit=0):
    count = lax.axis_size(axis)
    return lax.ppermute(block, axis, [(i, i ^ (1 << bit)) for i in range(count)])


def from_chunk(block, distance):
    axes = ("seq", "mp")
    count = lax.axis_size("seq") * lax.axis_size("mp")
    return lax.ppermute(block, axes, [(i + distance, i) for i in range(count) if 0 <= i + distance < count])


def pick(array, index, dim):
    return lax.dynamic_index_in_dim(array, index, dim, keepdims=False)


def bits_of(axis):
    return lax.axis_size(axis).bit_length() - 1


def reduce_bit(parts, dim, axis, bit):
    mine = (lax.axis_index(axis) >> bit) & 1
    got = swapped(pick(parts, 1 - mine, dim), axis, bit)
    return low(pick(parts, mine, dim).astype(f32) + got.astype(f32))


def reduce_axis(parts, dim, axis):
    count = lax.axis_size(axis)
    for bit in range(bits_of(axis)):
        low_count = parts.shape[dim] // 2
        shaped = parts.reshape(parts.shape[:dim] + (low_count, 2) + parts.shape[dim + 1 :])
        parts = reduce_bit(shaped, dim + 1, axis, bit)
    return parts.reshape(parts.shape[:dim] + parts.shape[dim + 1 :])


def gather_quarters(quarter, shape):
    first = swapped(quarter, "mp")
    seq_bit = lax.axis_index("seq") & 1
    pipe = lax.axis_index("pipe")
    me = 2 * seq_bit + pipe
    second = swapped(first, "seq")
    third = swapped(jnp.stack([first, second]), "pipe")
    full = jnp.zeros((4,) + quarter.shape, quarter.dtype)
    for block, place in ((first, me), (second, me ^ 2), (third[0], me ^ 1), (third[1], me ^ 3)):
        full = lax.dynamic_update_slice_in_dim(full, block[None], place, 0)
    return full.reshape(shape)


def in_order(first, mine, recv, axis):
    return jnp.where(
        first == 0, jnp.concatenate([mine, recv], axis=axis), jnp.concatenate([recv, mine], axis=axis)
    )


def summed(vectors):
    return jnp.sum(lax.all_gather(vectors, ("pipe", "dp", "seq", "mp")), axis=0)


def on_device(
    characters,
    row_lengths,
    w_query,
    b_query,
    w_key,
    w_value,
    b_value,
    w_attn_out,
    b_attn_out,
    gain_one,
    shift_one,
    w_inner,
    b_inner,
    w_outer,
    b_outer,
    gain_two,
    shift_two,
    w_conv,
    b_conv,
    gain_three,
    shift_three,
    molecule_grad,
):
    pipe = lax.axis_index("pipe")
    seq = lax.axis_index("seq")
    mp = lax.axis_index("mp")
    all_rows, span, half_model = characters.shape
    rows = all_rows // 2
    model = 2 * half_model
    local = w_query.shape[1]
    units = w_inner.shape[1]
    tokens = rows * span
    mols = tokens // KERNEL
    block = min(WINDOW, span)
    tile = min(256, tokens)
    own_start = (seq * lax.axis_size("mp") + mp) * span

    def line(vector):
        return vector.astype(f32)[None, :]

    def rows_of(array, index):
        return lax.dynamic_slice_in_dim(array, index * rows, rows, 0)

    chars = in_order(pipe, rows_of(characters, pipe), swapped(rows_of(characters, 1 - pipe), "pipe"), 2)
    mol_grad = in_order(pipe, rows_of(molecule_grad, pipe), swapped(rows_of(molecule_grad, 1 - pipe), "pipe"), 2)
    mol_grad = mol_grad.reshape(mols, model)

    me = 2 * (seq & 1) + pipe
    w4 = jnp.stack([w_query, w_key, w_value, w_attn_out.T])
    w4_other = gather_quarters(pick(w4, me, 0), w4.shape)
    inner_other = gather_quarters(pick(w_inner.reshape(4, model // 4, units), me, 0), w_inner.shape)
    outer_other = gather_quarters(pick(w_outer.reshape(4, units // 4, model), me, 0), w_outer.shape)
    small = jnp.concatenate([b_query, b_value, b_inner]).astype(f32)[None, :]
    small_other = swapped(small, "mp")
    bq = (small[:, :local], small_other[:, :local])
    bv = (small[:, local : 2 * local], small_other[:, local : 2 * local])
    bi = (small[:, 2 * local :], small_other[:, 2 * local :])

    hops = -(-WINDOW // span)
    pieces = [chars]
    for hop in range(1, hops + 1):
        width = min(span, WINDOW - (hop - 1) * span)
        pieces.insert(0, from_chunk(chars[:, span - width :], -hop))
        pieces.append(from_chunk(chars[:, :width], hop))
    x_ext = jnp.concatenate(pieces, axis=1)

    lengths = rows_of(row_lengths, pipe)
    info = jnp.concatenate([own_start[None].astype(jnp.int32), lengths])
    positions = own_start + jnp.arange(span, dtype=jnp.int32)
    live = (positions[None, :] < lengths[:, None]).astype(f32).reshape(tokens, 1)
    live_mols = live.reshape(mols, KERNEL)[:, :1]
    live = jnp.broadcast_to(live, (tokens, PAIR))
    live_mols = jnp.broadcast_to(live_mols, (mols, PAIR))

    q_own, k_own, v_own, att_own, lse_own, part = attend(info, x_ext, w4, bq[0], bv[0], span, block)
    q_other, k_other, v_other, att_other, lse_other, n1, scale1, middle = attend(
        info, x_ext, w4_other, bq[1], bv[1], span, block, (part, line(b_attn_out), line(gain_one), line(shift_one))
    )
    n1, scale1, middle = (a.reshape(tokens, -1) for a in (n1, scale1, middle))
    act_own, slope_own, part = feed(middle, w_inner, w_outer, bi[0], tile)
    act_other, slope_other, n2, scale2, sent = feed(
        middle,
        inner_other,
        outer_other,
        bi[1],
        tile,
        (part, n1, live, line(gain_one), line(shift_one), line(b_outer), line(gain_two), line(shift_two)),
    )
    mol_out, grad_conv, grouped, grad_two, grad_feed, vec_conv = conv(
        sent,
        w_conv.reshape(KERNEL, model, model),
        line(b_conv),
        line(gain_three),
        line(shift_three),
        line(gain_two),
        mol_grad,
        live_mols,
        n2,
        scale2,
        live,
        2,
    )

    mine_side = pipe.astype(jnp.int32)[None]
    their_side = 1 - mine_side

    def over_pipe(product):
        return product(mine_side, swapped(product(their_side, None), "pipe"))

    dp_size, seq_size, mp_size = (lax.axis_size(a) for a in ("dp", "seq", "mp"))
    conv_part = over_pipe(lambda side, got: conv_weight(side, grouped, grad_conv, got))
    conv_part = conv_part.reshape(dp_size, seq_size, mp_size, -1, model)
    conv_part = reduce_axis(conv_part, 0, "dp")
    conv_part = reduce_axis(conv_part, 0, "seq")
    grad_w_conv = reduce_axis(conv_part, 0, "mp")

    outer_part = over_pipe(lambda side, got: weight(side, grad_feed, act_own, act_other, got))

    gh_own, gh_other, grad_one, grad_branch, vec_one, bi_own, bi_other = feed_back(
        grad_feed,
        grad_two,
        (slope_own, slope_other),
        n1,
        scale1,
        (w_outer, outer_other),
        (w_inner, inner_other),
        line(gain_one),
        tile,
    )
    inner_part = over_pipe(lambda side, got: weight(side, middle, gh_own, gh_other, got))

    def head_rows(part, axes):
        part = part.reshape(2, dp_size, seq_size, -1, part.shape[2])
        dims = ["mp", "dp", "seq"]
        for axis in axes:
            dim = dims.index(axis)
            if axis == "mp":
                part = low(part[0].astype(f32) + swapped(part[1], "mp").astype(f32))
            else:
                part = reduce_axis(part, dim, axis)
            dims.remove(axis)
        return part

    outer_sum = head_rows(outer_part, ("seq", "mp", "dp"))
    inner_sum = head_rows(inner_part, ("mp", "seq", "dp"))

    grad_branch = grad_branch.reshape(rows, span, model)
    grad_one = grad_one.reshape(rows, span, model)
    back_other = attend_back(info, grad_branch, w4_other, q_other, k_other, v_other, lse_other, block)
    back_own = attend_back(info, grad_branch, w4, q_own, k_own, v_own, lse_own, block)
    head_part = over_pipe(
        lambda side, got: project_weight(
            side, x_ext, grad_branch, (*back_own, att_own), (*back_other, att_other), span, got
        )
    )
    head_sum = head_rows(head_part, ("mp", "seq", "dp"))
    center, left, right, vec_late = input_back(grad_one, back_own, back_other, w4, w4_other, span)

    for hop in range(1, hops + 1):
        width = min(span, WINDOW - (hop - 1) * span)
        top = WINDOW - (hop - 1) * span
        to_tail = from_chunk(left[:, top - width : top], hop).astype(f32)
        to_head = from_chunk(right[:, WINDOW - top : WINDOW - top + width], -hop).astype(f32)
        pad = ((0, 0), (0, span - width), (0, 0))
        center = center + jnp.pad(to_head, pad) + jnp.pad(to_tail, (pad[0], pad[1][::-1], pad[2]))
    center = center.reshape(rows, span, 2, half_model)
    chars_got = swapped(low(pick(center, 1 - pipe, 2)), "pipe").astype(f32)
    chars_grad = in_order(pipe, pick(center, pipe, 2), chars_got, 0)
    mol_out = mol_out.reshape(rows, span // KERNEL, 2, half_model)
    mol_got = swapped(pick(mol_out, 1 - pipe, 2), "pipe")
    molecules = in_order(pipe, pick(mol_out, pipe, 2), mol_got, 0)

    inner_vec = in_order(mp, bi_own[:1], bi_other[:1], 1).reshape(-1, model)
    early = summed(jnp.concatenate([vec_conv[:6], vec_one[:3], inner_vec], axis=0))
    late = summed(in_order(mp, vec_late[:2], vec_late[2:4], 1))
    grad_b_conv, grad_gain_three, grad_shift_three, grad_gain_two, grad_shift_two, grad_b_outer = early[:6]
    grad_b_attn_out, grad_gain_one, grad_shift_one = early[6:9]
    grad_b_inner = early[9:].reshape(-1)

    head_sum = head_sum.astype(f32)
    grad_w_query, grad_w_key, grad_w_value, grad_w_attn = (
        head_sum[:, i * local : (i + 1) * local] for i in range(4)
    )
    return (
        molecules,
        chars_grad,
        grad_w_query,
        late[0],
        grad_w_key,
        grad_w_value,
        late[1],
        grad_w_attn.T,
        grad_b_attn_out,
        grad_gain_one,
        grad_shift_one,
        inner_sum.astype(f32),
        grad_b_inner,
        outer_sum.astype(f32).T,
        grad_b_outer,
        grad_gain_two,
        grad_shift_two,
        grad_w_conv.astype(f32),
        grad_b_conv,
        grad_gain_three,
        grad_shift_three,
    )


def solution(mesh):
    return jax.shard_map(
        on_device,
        mesh=mesh,
        in_specs=(
            P("dp", ("seq", "mp"), "pipe"),
            P("dp"),
            P(None, "mp"),
            P("mp"),
            P(None, "mp"),
            P(None, "mp"),
            P("mp"),
            P("mp", None),
            P(),
            P(),
            P(),
            P(None, "mp"),
            P("mp"),
            P("mp", None),
            P(),
            P(),
            P(),
            P(),
            P(),
            P(),
            P(),
            P("dp", ("seq", "mp"), "pipe"),
        ),
        out_specs=(
            P("dp", ("seq", "mp"), "pipe"),
            P("dp", ("seq", "mp"), "pipe"),
            P(("pipe", "dp", "seq"), "mp"),
            P(),
            P(("pipe", "dp", "seq"), "mp"),
            P(("pipe", "dp", "seq"), "mp"),
            P(),
            P("mp", ("pipe", "dp", "seq")),
            P(),
            P(),
            P(),
            P(("pipe", "dp", "seq"), "mp"),
            P(),
            P("mp", ("pipe", "dp", "seq")),
            P(),
            P(),
            P(),
            P(("pipe", "dp", "seq", "mp"), None),
            P(),
            P(),
            P(),
        ),
        check_vma=False,
    )
```

time: 2120 us -> 518 us (0.24)
  waiting for transfers between devices: 646 us -> 85.5 us
  matrix products: 528 us -> 0 us
  local copies, waits for them, and re-layouts: 464 us -> 68.2 us
  other arithmetic: 348 us -> 32.5 us
  Pallas kernels: 0 us -> 202 us
  blocking collectives: 41.3 us -> 70.5 us
    dot_general x68 -> x0, matrix products: 484 us -> none  [the longest x16 106 us: apply_right(): jnp.einsum('bsi,ij->bsj', left, right, preferred_element_type=jnp.float32)]
    reduce_scatter x23 -> x0, waiting for transfers between devices: 464 us -> none  [the longest x1 141 us: on_device(): lax.psum_scatter(conv_term, ('pipe', 'dp', 'seq', 'mp'), scatter_dimensio...]
    pallas_call x0 -> x17, Pallas kernels: none -> 202 us  [call(): pl.pallas_call(body, grid_spec=pltpu.PrefetchScalarGridSpec(num_scalar_pr...]
    another operation x42 -> x1, local copies, waits for them, and re-layouts: 128 us -> 1.73 us  [on_device(): grad_b_conv, grad_gain_three, grad_shift_three, grad_gain_two, grad_shift...]
    reduce_sum x62 -> x2, other arithmetic: 123 us -> 2.21 us  [summed(): return jnp.sum(lax.all_gather(vectors, ('pipe', 'dp', 'seq', 'mp')), axis=0)]
    cond x316 -> x0, local copies, waits for them, and re-layouts: 118 us -> none
    slice x53 -> x12, local copies, waits for them, and re-layouts: 112 us -> 11.3 us  [the longest x2 4.59 us: head_rows(): part = low(part[0].astype(f32) + swapped(part[1], 'mp').astype(f32))]
    add x31 -> x3, other arithmetic: 83 us -> 1.4 us  [the longest x1 1.39 us: on_device(): center + jnp.pad(to_head, pad)]
  transfers between devices with their start and end apart: 73 -> 39, of which waited for: 36 -> 13; matrix products, arithmetic and copies ran while one was open for 61% -> 17% of each run, Pallas kernels for 0% -> 33%
where the time goes in v1:
time: 518 us; the launch traced here: 513 us
  Pallas kernels  202 us (39%)
  waiting for transfers between devices  85.5 us (17%)
  blocking collectives  70.5 us (14%)
  local copies, waits for them, and re-layouts  68.2 us (13%)
  starting transfers between devices  39.4 us (8%)
  other arithmetic  32.5 us (6%)
  between operations  14.9 us (3%)
    pallas_call x17, Pallas kernels, call(): pl.pallas_call(body, grid_spec=pltpu.PrefetchScalarGridSpec(num_scalar_pr...  202 us
    ppermute x34, waiting for transfers between devices, swapped(): return lax.ppermute(block, axis, [(i, i ^ 1 << bit) for i in range(count)])  80.3 us
    all_gather x1, blocking collectives, summed(): return jnp.sum(lax.all_gather(vectors, ('pipe', 'dp', 'seq', 'mp')), axis=0)  70.5 us
    ppermute x34, starting transfers between devices, swapped(): return lax.ppermute(block, axis, [(i, i ^ 1 << bit) for i in range(count)])  24.6 us
    ppermute x4, starting transfers between devices, from_chunk(): lax.ppermute(block, axes, [(i + distance, i) for i in range(count) if 0 <...  14.8 us
    broadcast_in_dim x9, local copies, waits for them, and re-layouts, line(): return vector.astype(f32)[None, :]  11.3 us
  transfers between devices with their start and end apart: 39, of which 13 were waited for; matrix products, arithmetic and copies ran while one was open for 17% of the time, Pallas kernels for 33%

profile of v1, /device:TPU:0, one launch (start us, length us, event | category | flops | bytes accessed | tf_op | source)
XLA Modules:
  0.0 512.9 jit_solution(16459991106503450208)
XLA Ops:
  11.3 3.0 collective-permute-start.3
  14.3 2.5 constant_dynamic-slice_fusion.13
  20.8 1.9 dynamic-slice_bitcast_fusion.2
  43.6 9.8 %collective-permute-done.10 = bf16[384,768]{1,0:T(8,128)(2,1)} collective-permute-done((bf16[384,768]{1,0:T(8,128)(2,1)}, bf16[384,768]{1,0:T(8,128)(2,1)}, u32[]{:S(2)}, u32[]{:S(2)}) %collective-permute-start.10) | collective-permute-done | bytes 589856 | tf_op jit(solution)/shard_map/ppermute | solution.py:641
  59.6 3.4 collective-permute-start.1
  64.5 2.3 pad_maximum_fusion.2
  66.8 1.9 collective-permute-done.8
  68.7 2.2 pad_maximum_fusion.3
  70.9 10.5 %collective-permute-done.11 = bf16[384,768]{1,0:T(8,128)(2,1)S(1)} collective-permute-done((bf16[384,768]{1,0:T(8,128)(2,1)}, bf16[384,768]{1,0:T(8,128)(2,1)S(1)}, u32[]{:S(2)}, u32[]{:S(2)}) %collective-permute-start.11) | collective-permute-done | bytes 589856 | tf_op jit(solution)/shard_map/ppermute | solution.py:641
  81.4 2.2 pad_maximum_fusion.4
  85.4 17.3 %shard_map.373 = (bf16[2,512,384]{2,1,0:T(8,128)(2,1)}, bf16[2,768,384]{2,1,0:T(8,128)(2,1)}, bf16[2,768,384]{2,1,0:T(8,128)(2,1)}, bf16[2,512,384]{2,1,0:T(8,12...) custom-call(s32[3]{0:T(128)} %pad_add_fusion.info_ref, bf16[2,768,768]{2,1,0:T(8,128)(2,1)} %pad_maximum_fusion.x_ref, ...), custom_call_target="tpu_custom_call" | custom-call | flops 12683575296 | bytes 9437184 | tf_op jit(solution)/shard_map/pallas_call | solution.py:64
  106.5 19.2 %shard_map.374 = (bf16[2,512,384]{2,1,0:T(8,128)(2,1)}, bf16[2,768,384]{2,1,0:T(8,128)(2,1)}, bf16[2,768,384]{2,1,0:T(8,128)(2,1)}, bf16[2,512,384]{2,1,0:T(8,12...) custom-call(s32[3]{0:T(128)} %pad_add_fusion.info_ref, ...), custom_call_target="tpu_custom_call" | custom-call | flops 12683575296 | bytes 9437184 | tf_op jit(solution)/shard_map/pallas_call | solution.py:64
  128.0 14.1 %shard_map.375 = (bf16[1024,1536]{1,0:T(8,128)(2,1)}, bf16[1024,1536]{1,0:T(8,128)(2,1)}, f32[1024,768]{1,0:T(8,128)}) custom-call(bf16[1024,768]{1,0:T(8,128)(2,1)} %bitcast.155, bf16[768,1536]{1,0:T(8,128)(2,1)} %wi_own.1, bf16[1536,768]{1,0:T(8,128)(2,1)} %wo_own.1, f32[1,1536]{1,0:T(1,128)} %slice.167.bi_ref), custom_call_target="tpu_custom_call" | custom-call | flops 7247757312 | bytes 12582912 | tf_op jit(solution)/shard_map/pallas_call | solution.py:64
  145.9 15.3 %shard_map.376 = (bf16[1024,1536]{1,0:T(8,128)(2,1)}, bf16[1024,1536]{1,0:T(8,128)(2,1)}, f32[1024,768]{1,0:T(8,128)}, f32[1024,128]{1,0:T(8,128)}, f32[6,1024,128]{2,1,0:T(8,128)}) custom-call(bf16[1024,768]{1,0:T(8,128)(2,1)} %bitcast.156, bf16[768,1536]{1,0:T(8,128)(2,1)} %bitcast.173, bf16[1536,768]{1,0:T(8,128)(2,1)} %bitcast.171, ...), custom_call_target="tpu_custom_call" | custom-call | flops 7247757312 | bytes 12582912 | tf_op jit(solution)/shard_map/pallas_call | solution.py:64
  162.0 13.6 %shard_map.377 = (bf16[256,768]{1,0:T(8,128)(2,1)}, bf16[256,768]{1,0:T(8,128)(2,1)}, bf16[4,256,768]{2,1,0:T(8,128)(2,1)}, f32[1024,768]{1,0:T(8,128)}, bf16[1024,768]{1,0:T(8,128)(2,1)}, /*index=5*/f32[8,768]{1,0:T(8,128)}) custom-call(f32[6,1024,128]{2,1,0:T(8,128)} %get-tuple-element.70.sent_ref, bf16[4,768,768]{2,1,0:T(8,128)(2,1)} %bitcast.194, ...), custom_call_target="tpu_custom_call" | custom-call | flops 3623878656 | bytes 23592960 | tf_op jit(solution)/shard_map/pallas_call | solution.py:64
  175.5 3.3 shard_map.388
  179.3 6.6 %shard_map.386 = bf16[2,384,1536]{2,1,0:T(8,128)(2,1)} custom-call(s32[1]{0:T(128)S(6)} %sub.13.side_ref, bf16[1024,768]{1,0:T(8,128)(2,1)} %get-tuple-element.74.gf_ref.left_ref, bf16[1024,1536]{1,0:T(8,128)(2,1)} %get-tuple-element.107.refs_0_, bf16[1024,1536]{1,0:T(8,128)(2,1)} %get-tuple-element.108.refs_1_), custom_call_target="tpu_custom_call" | custom-call | flops 2415919104 | bytes 11010048 | tf_op jit(solution)/shard_map/pallas_call | solution.py:64
  186.0 20.7 %shard_map.378 = (bf16[1024,1536]{1,0:T(8,128)(2,1)}, bf16[1024,1536]{1,0:T(8,128)(2,1)}, f32[1024,768]{1,0:T(8,128)}, bf16[1024,768]{1,0:T(8,128)(2,1)}, f32[8,...) custom-call(bf16[1024,768]{1,0:T(8,128)(2,1)} %get-tuple-element.74.gf_ref.left_ref, ...), custom_call_target="tpu_custom_call" | custom-call | flops 11596411904 | bytes 12582912 | tf_op jit(solution)/shard_map/pallas_call | solution.py:64
  206.7 6.6 %shard_map.384 = bf16[2,384,1536]{2,1,0:T(8,128)(2,1)} custom-call(s32[1]{0:T(128)S(6)} %sub.13.side_ref, bf16[1024,768]{1,0:T(8,128)(2,1)} %bitcast.157, bf16[1024,1536]{1,0:T(8,128)(2,1)} %get-tuple-element.105.refs_0_, bf16[1024,1536]{1,0:T(8,128)(2,1)} %get-tuple-element.106.refs_1_), custom_call_target="tpu_custom_call" | custom-call | flops 2415919104 | bytes 11010048 | tf_op jit(solution)/shard_map/pallas_call | solution.py:64
  216.2 16.9 %shard_map.380 = (bf16[2,512,384]{2,1,0:T(8,128)(2,1)}, bf16[2,768,384]{2,1,0:T(8,128)(2,1)}, bf16[2,768,384]{2,1,0:T(8,128)(2,1)}) custom-call(s32[3]{0:T(128)} %pad_add_fusion.info_ref, bf16[2,512,768]{2,1,0:T(8,128)(2,1)} %bitcast.160, bf16[4,768,384]{2,1,0:T(8,128)(2,1)} %copy-done.7, bf16[2,512,384]{2,1,0:T(8,128)(2,1)} %get-tuple-element.88.q_ref, ...), custom_call_target="tpu_custom_call" | custom-call | flops 6341787648 | bytes 9437184 | tf_op jit(solution)/shard_map/pallas_call | solution.py:64
  233.2 17.1 %shard_map.379 = (bf16[2,512,384]{2,1,0:T(8,128)(2,1)}, bf16[2,768,384]{2,1,0:T(8,128)(2,1)}, bf16[2,768,384]{2,1,0:T(8,128)(2,1)}) custom-call(s32[3]{0:T(128)} %pad_add_fusion.info_ref, bf16[2,512,768]{2,1,0:T(8,128)(2,1)} %bitcast.161, bf16[4,768,384]{2,1,0:T(8,128)(2,1)} %copy-done.4, bf16[2,512,384]{2,1,0:T(8,128)(2,1)} %get-tuple-element.81.q_ref, ...), custom_call_target="tpu_custom_call" | custom-call | flops 6341787648 | bytes 9437184 | tf_op jit(solution)/shard_map/pallas_call | solution.py:64
  250.2 12.5 %shard_map.381 = (f32[2,512,768]{2,1,0:T(8,128)}, bf16[2,128,768]{2,1,0:T(8,128)(2,1)}, bf16[2,128,768]{2,1,0:T(8,128)(2,1)}, f32[8,384]{1,0:T(8,128)}) custom-call(f32[2,512,768]{2,1,0:T(8,128)} %bitcast.197, bf16[2,512,384]{2,1,0:T(8,128)(2,1)} %get-tuple-element.85.refs_0_, bf16[2,768,384]{2,1,0:T(8,128)(2,1)} %get-tuple-element.86.refs_1_, ...), custom_call_target="tpu_custom_call" | custom-call | flops 5435817984 | bytes 14155776 | tf_op jit(solution)/shard_map/pallas_call | solution.py:64
  262.7 8.6 %collective-permute-start.15 = (bf16[2,128,768]{2,1,0:T(8,128)(2,1)}, bf16[2,128,768]{2,1,0:T(8,128)(2,1)S(1)}, u32[]{:S(2)}, u32[]{:S(2)}) collective-permute-start(bf16[2,128,768]{2,1,0:T(8,128)(2,1)} %get-tuple-element.96), channel_id=1, source_target_pairs={{0,1},{1,2},{2,3},{4,5},{5,6},{6,7},{8,9},{9,10},{10,11},{12,13},{... | collective-permute-start | bytes 1179656 | tf_op jit(solution)/shard_map/ppermute | solution.py:647
  272.7 9.6 %shard_map.382 = bf16[2,384,1536]{2,1,0:T(8,128)(2,1)} custom-call(s32[1]{0:T(128)S(6)} %sub.13.side_ref, bf16[2,768,768]{2,1,0:T(8,128)(2,1)} %pad_maximum_fusion.x_ref, bf16[2,512,768]{2,1,0:T(8,128)(2,1)} %bitcast.162, bf16[2,512,384]{2,1,0:T(8,128)(2,1)} %get-tuple-element.85.refs_0_, bf16[2,768,384]{2,1,0:T(8,128)(2,1)} %get-tuple-element.86.refs_1_, ...), custom_call_target="tpu_custom_call" | custom-call | flops 3623878656 | bytes 14155776 | tf_op jit(solution)/shard_map/pallas_call | solution.py:64
  283.8 5.2 %collective-permute-done.15 = bf16[2,128,768]{2,1,0:T(8,128)(2,1)S(1)} collective-permute-done((bf16[2,128,768]{2,1,0:T(8,128)(2,1)}, bf16[2,128,768]{2,1,0:T(8,128)(2,1)S(1)}, u32[]{:S(2)}, u32[]{:S(2)}) %collective-permute-start.15) | collective-permute-done | bytes 393248 | tf_op jit(solution)/shard_map/ppermute | solution.py:647
  291.3 2.9 reshape.369
  294.2 3.3 constant_dynamic-slice_fusion.6
  299.7 70.5 %all_gather.10 = f32[32,2,768]{2,1,0:T(2,128)S(1)} all-gather(f32[1,2,768]{2,1,0:T(2,128)S(1)} %maximum_select_fusion.4), channel_id=1, replica_groups=mesh['pipe'=2,'dp'=4,'seq'=2,'mp'=2] {'pipe','dp','seq','mp'}, dimensions={0}, use_global_device_ids=true | all-gather | bytes 202752 | tf_op jit(solution)/shard_map/all_gather | solution.py:693
  370.9 2.0 maximum_select_fusion.3
  377.8 3.8 shard_map.389
  381.6 2.3 dynamic-slice_bitcast_fusion
  384.0 7.7 %shard_map.387 = bf16[2,384,1536]{2,1,0:T(8,128)(2,1)} custom-call(s32[1]{0:T(128)} %bitcast.32.side_ref, bf16[1024,768]{1,0:T(8,128)(2,1)} %get-tuple-element.74.gf_ref.left_ref, bf16[1024,1536]{1,0:T(8,128)(2,1)} %get-tuple-element.107.refs_0_, bf16[1024,1536]{1,0:T(8,128)(2,1)} %get-tuple-element.108.refs_1_, ...), custom_call_target="tpu_custom_call" | custom-call | flops 2415919104 | bytes 11010048 | tf_op jit(solution)/shard_map/pallas_call | solution.py:64
  391.6 2.4 dynamic-slice_bitcast_fusion.1
  394.1 7.7 %shard_map.385 = bf16[2,384,1536]{2,1,0:T(8,128)(2,1)} custom-call(s32[1]{0:T(128)} %bitcast.32.side_ref, bf16[1024,768]{1,0:T(8,128)(2,1)} %bitcast.158, bf16[1024,1536]{1,0:T(8,128)(2,1)} %get-tuple-element.105.refs_0_, bf16[1024,1536]{1,0:T(8,128)(2,1)} %get-tuple-element.106.refs_1_, bf16[2,384,1536]{2,1,0:T(8,128)(2,1)} %collective-permute-done.23.refs_2_), custom_call_target="tpu_custom_call" | custom-call | flops 2415919104 | bytes 11010048 | tf_op jit(solution)/shard_map/pallas_call | solution.py:64
  404.6 9.8 %shard_map.383 = bf16[2,384,1536]{2,1,0:T(8,128)(2,1)} custom-call(s32[1]{0:T(128)} %bitcast.32.side_ref, bf16[2,768,768]{2,1,0:T(8,128)(2,1)} %pad_maximum_fusion.x_ref, bf16[2,512,768]{2,1,0:T(8,128)(2,1)} %bitcast.163, bf16[2,512,384]{2,1,0:T(8,128)(2,1)} %get-tuple-element.85.refs_0_, bf16[2,768,384]{2,1,0:T(8,128)(2,1)} %get-tuple-element.86.refs_1_, ...), custom_call_target="tpu_custom_call" | custom-call | flops 3623878656 | bytes 14155776 | tf_op jit(solution)/shard_map/pallas_call | solution.py:64
  414.4 2.8 fusion.21
  418.3 2.0 collective-permute-start.19
  420.3 2.1 reduce_sum.19
  430.8 3.0 collective-permute-done.24
  435.5 2.1 collective-permute-start.25
  437.6 21.4 %collective-permute-done.19 = bf16[4,2,48,1536]{3,2,0,1:T(8,128)(2,1)} collective-permute-done((bf16[4,2,48,1536]{3,2,0,1:T(8,128)(2,1)}, bf16[4,2,48,1536]{3,2,0,1:T(8,128)(2,1)}, u32[]{:S(2)}, u32[]{:S(2)}) %collective-permute-start.19) | collective-permute-done | bytes 1179680 | tf_op jit(solution)/shard_map/ppermute | solution.py:641
  460.7 2.1 collective-permute-start.20
  463.1 7.7 %collective-permute-done.30 = bf16[4,48,1536]{2,1,0:T(8,128)(2,1)S(1)} collective-permute-done((bf16[4,48,1536]{2,1,0:T(8,128)(2,1)S(1)}, bf16[4,48,1536]{2,1,0:T(8,128)(2,1)S(1)}, u32[]{:S(2)}, u32[]{:S(2)}) %collective-permute-start.30) | collective-permute-done | bytes 589856 | tf_op jit(solution)/shard_map/ppermute | solution.py:641
  473.3 3.8 collective-permute-done.20
  477.2 2.0 collective-permute-start.21
  481.7 10.0 %collective-permute-done.26 = bf16[2,48,1536]{2,1,0:T(8,128)(2,1)S(1)} collective-permute-done((bf16[2,48,1536]{2,1,0:T(8,128)(2,1)S(1)}, bf16[2,48,1536]{2,1,0:T(8,128)(2,1)S(1)}, u32[]{:S(2)}, u32[]{:S(2)}) %collective-permute-start.26) | collective-permute-done | bytes 294944 | tf_op jit(solution)/shard_map/ppermute | solution.py:641
  491.9 5.9 %collective-permute-done.21 = bf16[2,48,1536]{2,1,0:T(8,128)(2,1)S(1)} collective-permute-done((bf16[2,48,1536]{2,1,0:T(8,128)(2,1)S(1)}, bf16[2,48,1536]{2,1,0:T(8,128)(2,1)S(1)}, u32[]{:S(2)}, u32[]{:S(2)}) %collective-permute-start.21) | collective-permute-done | bytes 294944 | tf_op jit(solution)/shard_map/ppermute | solution.py:641
  500.7 3.7 collective-permute-done.22
  (209 shorter events, 90.7 us)
Async XLA Ops:
  7.2 413.1 %all-gather.4.cloned.1.call-start = ((), (), s32[]{:S(2)}) async-start(), calls=%async_computation | async-start | bytes 1622016 | tf_op jit(solution)/shard_map/all_gather | solution.py:693
  11.3 28.4 %collective-permute-start.3 = (bf16[768,384]{1,0:T(8,128)(2,1)}, bf16[768,384]{1,0:T(8,128)(2,1)}, u32[]{:S(2)}, u32[]{:S(2)}) collective-permute-start(bf16[768,384]{1,0:T(8,128)(2,1)} %dynamic-slice_bitcast_fusion.4), channel_id=1, source_target_pairs={{0,1},{1,0},{2,3},{3,2},{4,5},{5,4},{6,7},{7,6},{8,9},{9,8},{10,11... | collective-permute-start | bytes 1769480 | tf_op jit(solution)/shard_map/ppermute | solution.py:641
  14.3 8.6 %copy-start.19 = (s32[4]{0:T(128)S(1)}, s32[4]{0:T(128)}, u32[]{:S(2)}) copy-start(s32[4]{0:T(128)} %param.23) | copy-start | bytes 52
  14.3 9.4 %copy-start.11 = (bf16[4,128,384]{2,1,0:T(8,128)(2,1)S(1)}, bf16[4,128,384]{2,1,0:T(8,128)(2,1)}, u32[]{:S(2)}) copy-start(bf16[4,128,384]{2,1,0:T(8,128)(2,1)} %param.43) | copy-start | bytes 1179652
  16.8 40.9 %collective-permute-start = (bf16[2,512,384]{2,1,0:T(8,128)(2,1)}, bf16[2,512,384]{2,1,0:T(8,128)(2,1)}, u32[]{:S(2)}, u32[]{:S(2)}) collective-permute-start(bf16[2,512,384]{2,1,0:T(8,128)(2,1)} %get-tuple-element.129), channel_id=1, source_target_pairs={{0,16},{16,0},{1,17},{17,1},{2,18},{18,2},{3,19},{19,3},{4,20},{20... | collective-permute-start | bytes 2359304 | tf_op jit(solution)/shard_map/ppermute | solution.py:641
  16.8 19.5 %collective-permute-start.6 = (f32[1,2304]{1,0:T(1,128)S(1)}, f32[1,2304]{1,0:T(1,128)}, u32[]{:S(2)}, u32[]{:S(2)}) collective-permute-start(f32[1,2304]{1,0:T(1,128)S(1)} %maximum_convert_fusion), channel_id=1, source_target_pairs={{0,1},{1,0},{2,3},{3,2},{4,5},{5,4},{6,7},{7,6},{8,9},{9,8},{10,11... | collective-permute-start | bytes 27656 | tf_op jit(solution)/shard_map/ppermute | solution.py:641
  18.9 24.1 %collective-permute-start.7 = (bf16[192,1536]{1,0:T(8,128)(2,1)}, bf16[192,1536]{1,0:T(8,128)(2,1)}, u32[]{:S(2)}, u32[]{:S(2)}) collective-permute-start(bf16[192,1536]{1,0:T(8,128)(2,1)} %dynamic-slice_bitcast_fusion.3), channel_id=1, source_target_pairs={{0,1},{1,0},{2,3},{3,2},{4,5},{5,4},{6,7},{7,6},{8,9},{9,8},{10,11... | collective-permute-start | bytes 1769480 | tf_op jit(solution)/shard_map/ppermute | solution.py:641
  22.8 30.6 %collective-permute-start.10 = (bf16[384,768]{1,0:T(8,128)(2,1)}, bf16[384,768]{1,0:T(8,128)(2,1)}, u32[]{:S(2)}, u32[]{:S(2)}) collective-permute-start(bf16[384,768]{1,0:T(8,128)(2,1)} %dynamic-slice_bitcast_fusion.2), channel_id=1, source_target_pairs={{0,1},{1,0},{2,3},{3,2},{4,5},{5,4},{6,7},{7,6},{8,9},{9,8},{10,11... | collective-permute-start | bytes 1769480 | tf_op jit(solution)/shard_map/ppermute | solution.py:641
  36.3 2.5 collective-permute-start.13
  39.7 24.8 %collective-permute-start.4 = (bf16[768,384]{1,0:T(8,128)(2,1)}, bf16[768,384]{1,0:T(8,128)(2,1)S(1)}, u32[]{:S(2)}, u32[]{:S(2)}) collective-permute-start(bf16[768,384]{1,0:T(8,128)(2,1)} %collective-permute-done.3), channel_id=1, source_target_pairs={{0,2},{2,0},{1,3},{3,1},{4,6},{6,4},{5,7},{7,5},{8,10},{10,8},{9,1... | collective-permute-start | bytes 1769480 | tf_op jit(solution)/shard_map/ppermute | solution.py:641
  43.0 25.8 %collective-permute-start.8 = (bf16[192,1536]{1,0:T(8,128)(2,1)}, bf16[192,1536]{1,0:T(8,128)(2,1)S(1)}, u32[]{:S(2)}, u32[]{:S(2)}) collective-permute-start(bf16[192,1536]{1,0:T(8,128)(2,1)} %collective-permute-done.7), channel_id=1, source_target_pairs={{0,2},{2,0},{1,3},{3,1},{4,6},{6,4},{5,7},{7,5},{8,10},{10,8},{9,1... | collective-permute-start | bytes 1769480 | tf_op jit(solution)/shard_map/ppermute | solution.py:641
  53.4 28.0 %collective-permute-start.11 = (bf16[384,768]{1,0:T(8,128)(2,1)}, bf16[384,768]{1,0:T(8,128)(2,1)S(1)}, u32[]{:S(2)}, u32[]{:S(2)}) collective-permute-start(bf16[384,768]{1,0:T(8,128)(2,1)} %collective-permute-done.10), channel_id=1, source_target_pairs={{0,2},{2,0},{1,3},{3,1},{4,6},{6,4},{5,7},{7,5},{8,10},{10,8},{9,1... | collective-permute-start | bytes 1769480 | tf_op jit(solution)/shard_map/ppermute | solution.py:641
  59.6 24.2 %collective-permute-start.1 = (bf16[2,128,768]{2,1,0:T(8,128)(2,1)S(1)}, bf16[2,128,768]{2,1,0:T(8,128)(2,1)S(1)}, u32[]{:S(2)}, u32[]{:S(2)}) collective-permute-start(bf16[2,128,768]{2,1,0:T(8,128)(2,1)S(1)} %get-tuple-element.126), channel_id=1, source_target_pairs={{0,1},{1,2},{2,3},{4,5},{5,6},{6,7},{8,9},{9,10},{10,11},{12,13},{... | collective-permute-start | bytes 1179656 | tf_op jit(solution)/shard_map/ppermute | solution.py:647
  63.1 20.7 %collective-permute-start.2 = (bf16[2,128,768]{2,1,0:T(8,128)(2,1)S(1)}, bf16[2,128,768]{2,1,0:T(8,128)(2,1)S(1)}, u32[]{:S(2)}, u32[]{:S(2)}) collective-permute-start(bf16[2,128,768]{2,1,0:T(8,128)(2,1)S(1)} %get-tuple-element.127), channel_id=1, source_target_pairs={{1,0},{2,1},{3,2},{5,4},{6,5},{7,6},{9,8},{10,9},{11,10},{13,12},{... | collective-permute-start | bytes 1179656 | tf_op jit(solution)/shard_map/ppermute | solution.py:647
  66.8 35.9 %collective-permute-start.5 = (bf16[2,768,384]{2,1,0:T(8,128)(2,1)}, bf16[2,768,384]{2,1,0:T(8,128)(2,1)}, u32[]{:S(2)}, u32[]{:S(2)}) collective-permute-start(bf16[2,768,384]{2,1,0:T(8,128)(2,1)} %pad_maximum_fusion.2), channel_id=1, source_target_pairs={{0,16},{16,0},{1,17},{17,1},{2,18},{18,2},{3,19},{19,3},{4,20},{20... | collective-permute-start | bytes 3538952 | tf_op jit(solution)/shard_map/ppermute | solution.py:641
  70.9 54.8 %collective-permute-start.9 = (bf16[2,192,1536]{2,1,0:T(8,128)(2,1)}, bf16[2,192,1536]{2,1,0:T(8,128)(2,1)}, u32[]{:S(2)}, u32[]{:S(2)}) collective-permute-start(bf16[2,192,1536]{2,1,0:T(8,128)(2,1)} %pad_maximum_fusion.3), channel_id=1, source_target_pairs={{0,16},{16,0},{1,17},{17,1},{2,18},{18,2},{3,19},{19,3},{4,20},{20... | collective-permute-start | bytes 3538952 | tf_op jit(solution)/shard_map/ppermute | solution.py:641
  83.6 58.5 %collective-permute-start.12 = (bf16[2,384,768]{2,1,0:T(8,128)(2,1)}, bf16[2,384,768]{2,1,0:T(8,128)(2,1)}, u32[]{:S(2)}, u32[]{:S(2)}) collective-permute-start(bf16[2,384,768]{2,1,0:T(8,128)(2,1)} %pad_maximum_fusion.4), channel_id=1, source_target_pairs={{0,16},{16,0},{1,17},{17,1},{2,18},{18,2},{3,19},{19,3},{4,20},{20... | collective-permute-start | bytes 3538952 | tf_op jit(solution)/shard_map/ppermute | solution.py:641
  127.9 14.1 %copy-start.8 = (bf16[4,192,1536]{2,1,0:T(8,128)(2,1)}, bf16[4,192,1536]{2,1,0:T(8,128)(2,1)S(1)}, u32[]{:S(2)}) copy-start(bf16[4,192,1536]{2,1,0:T(8,128)(2,1)S(1)} %slice_dynamic-update-slice_fusion.2) | copy-start | bytes 7077892
  178.8 199.0 %collective-permute-start.33 = (bf16[2,768,768]{2,1,0:T(8,128)(2,1)}, bf16[2,768,768]{2,1,0:T(8,128)(2,1)}, u32[]{:S(2)}, u32[]{:S(2)}) collective-permute-start(bf16[2,768,768]{2,1,0:T(8,128)(2,1)} %shard_map.388), channel_id=1, source_target_pairs={{0,16},{16,0},{1,17},{17,1},{2,18},{18,2},{3,19},{19,3},{4,20},{20... | collective-permute-start | bytes 7077896 | tf_op jit(solution)/shard_map/ppermute | solution.py:641
  186.0 198.0 %collective-permute-start.28 = (bf16[2,384,1536]{2,1,0:T(8,128)(2,1)}, bf16[2,384,1536]{2,1,0:T(8,128)(2,1)}, u32[]{:S(2)}, u32[]{:S(2)}) collective-permute-start(bf16[2,384,1536]{2,1,0:T(8,128)(2,1)} %shard_map.386), channel_id=1, source_target_pairs={{0,16},{16,0},{1,17},{17,1},{2,18},{18,2},{3,19},{19,3},{4,20},{20... | collective-permute-start | bytes 7077896 | tf_op jit(solution)/shard_map/ppermute | solution.py:641
  206.7 8.8 %copy-start.14 = (f32[8,768]{1,0:T(8,128)S(1)}, f32[8,768]{1,0:T(8,128)}, u32[]{:S(2)}) copy-start(f32[8,768]{1,0:T(8,128)} %get-tuple-element.102) | copy-start | bytes 73732
  206.7 8.8 %copy-start.13 = (f32[8,768]{1,0:T(8,128)S(1)}, f32[8,768]{1,0:T(8,128)}, u32[]{:S(2)}) copy-start(f32[8,768]{1,0:T(8,128)} %get-tuple-element.101) | copy-start | bytes 73732
  213.4 180.7 %collective-permute-start.23 = (bf16[2,384,1536]{2,1,0:T(8,128)(2,1)}, bf16[2,384,1536]{2,1,0:T(8,128)(2,1)}, u32[]{:S(2)}, u32[]{:S(2)}) collective-permute-start(bf16[2,384,1536]{2,1,0:T(8,128)(2,1)} %shard_map.384), channel_id=1, source_target_pairs={{0,16},{16,0},{1,17},{17,1},{2,18},{18,2},{3,19},{19,3},{4,20},{20... | collective-permute-start | bytes 7077896 | tf_op jit(solution)/shard_map/ppermute | solution.py:641
  250.2 22.4 %copy-start.12 = (bf16[256,768]{1,0:T(8,128)(2,1)S(1)}, bf16[256,768]{1,0:T(8,128)(2,1)}, u32[]{:S(2)}) copy-start(bf16[256,768]{1,0:T(8,128)(2,1)} %get-tuple-element.73) | copy-start | bytes 1179652
  262.7 26.3 %collective-permute-start.15 = (bf16[2,128,768]{2,1,0:T(8,128)(2,1)}, bf16[2,128,768]{2,1,0:T(8,128)(2,1)S(1)}, u32[]{:S(2)}, u32[]{:S(2)}) collective-permute-start(bf16[2,128,768]{2,1,0:T(8,128)(2,1)} %get-tuple-element.96), channel_id=1, source_target_pairs={{0,1},{1,2},{2,3},{4,5},{5,6},{6,7},{8,9},{9,10},{10,11},{12,13},{... | collective-permute-start | bytes 1179656 | tf_op jit(solution)/shard_map/ppermute | solution.py:647
  271.3 17.7 %collective-permute-start.16 = (bf16[2,128,768]{2,1,0:T(8,128)(2,1)}, bf16[2,128,768]{2,1,0:T(8,128)(2,1)S(1)}, u32[]{:S(2)}, u32[]{:S(2)}) collective-permute-start(bf16[2,128,768]{2,1,0:T(8,128)(2,1)} %get-tuple-element.97), channel_id=1, source_target_pairs={{1,0},{2,1},{3,2},{5,4},{6,5},{7,6},{9,8},{10,9},{11,10},{13,12},{... | collective-permute-start | bytes 1179656 | tf_op jit(solution)/shard_map/ppermute | solution.py:647
  272.7 17.2 %copy-start.5 = (f32[2,512,768]{2,1,0:T(8,128)S(1)}, f32[2,512,768]{2,1,0:T(8,128)}, u32[]{:S(2)}) copy-start(f32[2,512,768]{2,1,0:T(8,128)} %get-tuple-element.95) | copy-start | bytes 9437188
  289.0 115.6 %collective-permute-start.18 = (bf16[2,384,1536]{2,1,0:T(8,128)(2,1)}, bf16[2,384,1536]{2,1,0:T(8,128)(2,1)}, u32[]{:S(2)}, u32[]{:S(2)}) collective-permute-start(bf16[2,384,1536]{2,1,0:T(8,128)(2,1)} %shard_map.382), channel_id=1, source_target_pairs={{0,16},{16,0},{1,17},{17,1},{2,18},{18,2},{3,19},{19,3},{4,20},{20... | collective-permute-start | bytes 7077896 | tf_op jit(solution)/shard_map/ppermute | solution.py:641
  289.0 9.5 %collective-permute-start.14 = (bf16[2,128,384]{2,1,0:T(8,128)(2,1)}, bf16[2,128,384]{2,1,0:T(8,128)(2,1)}, u32[]{:S(2)}, u32[]{:S(2)}) collective-permute-start(bf16[2,128,384]{2,1,0:T(8,128)(2,1)} %bitcast.147), channel_id=1, source_target_pairs={{0,16},{16,0},{1,17},{17,1},{2,18},{18,2},{3,19},{19,3},{4,20},{20... | collective-permute-start | bytes 589832 | tf_op jit(solution)/shard_map/ppermute | solution.py:641
  297.5 75.4 %copy-start = (f32[2,512,2,384]{3,2,1,0:T(2,128)S(1)}, f32[2,512,2,384]{3,2,1,0:T(2,128)}, u32[]{:S(2)}) copy-start(f32[2,512,2,384]{3,2,1,0:T(2,128)} %reshape.369) | copy-start | bytes 9437188
  298.6 76.1 %collective-permute-start.17 = (bf16[2,512,384]{2,1,0:T(8,128)(2,1)}, bf16[2,512,384]{2,1,0:T(8,128)(2,1)}, u32[]{:S(2)}, u32[]{:S(2)}) collective-permute-start(bf16[2,512,384]{2,1,0:T(8,128)(2,1)} %bitcast.146), channel_id=1, source_target_pairs={{0,16},{16,0},{1,17},{17,1},{2,18},{18,2},{3,19},{19,3},{4,20},{20... | collective-permute-start | bytes 2359304 | tf_op jit(solution)/shard_map/ppermute | solution.py:641
  384.0 41.6 %collective-permute-start.34 = (bf16[2,2,2,96,768]{4,3,2,1,0:T(8,128)(2,1)}, bf16[2,2,2,96,768]{4,3,2,1,0:T(8,128)(2,1)}, u32[]{:S(2)}, u32[]{:S(2)}) collective-permute-start(bf16[2,2,2,96,768]{4,3,2,1,0:T(8,128)(2,1)} %dynamic-slice_bitcast_fusion), channel_id=1, source_target_pairs={{0,4},{4,0},{8,12},{12,8},{1,5},{5,1},{9,13},{13,9},{2,6},{6,2},{1... | collective-permute-start | bytes 3538952 | tf_op jit(solution)/shard_map/ppermute | solution.py:641
  394.1 33.4 %collective-permute-start.29 = (bf16[2,4,1,48,1536]{4,3,1,2,0:T(8,128)(2,1)}, bf16[2,4,1,48,1536]{4,3,1,2,0:T(8,128)(2,1)}, u32[]{:S(2)}, u32[]{:S(2)}) collective-permute-start(bf16[2,4,1,48,1536]{4,3,1,2,0:T(8,128)(2,1)} %dynamic-slice_bitcast_fusion.1), channel_id=1, source_target_pairs={{0,2},{2,0},{1,3},{3,1},{4,6},{6,4},{5,7},{7,5},{8,10},{10,8},{9,1... | collective-permute-start | bytes 3538952 | tf_op jit(solution)/shard_map/ppermute | solution.py:641
  404.6 29.1 %collective-permute-start.24 = (bf16[4,2,48,1536]{3,2,0,1:T(8,128)(2,1)}, bf16[4,2,48,1536]{3,2,0,1:T(8,128)(2,1)}, u32[]{:S(2)}, u32[]{:S(2)}) collective-permute-start(bf16[4,2,48,1536]{3,2,0,1:T(8,128)(2,1)} %copy.63), channel_id=1, source_target_pairs={{0,1},{1,0},{2,3},{3,2},{4,5},{5,4},{6,7},{7,6},{8,9},{9,8},{10,11... | collective-permute-start | bytes 3538952 | tf_op jit(solution)/shard_map/ppermute | solution.py:641
  418.3 40.8 %collective-permute-start.19 = (bf16[4,2,48,1536]{3,2,0,1:T(8,128)(2,1)}, bf16[4,2,48,1536]{3,2,0,1:T(8,128)(2,1)}, u32[]{:S(2)}, u32[]{:S(2)}) collective-permute-start(bf16[4,2,48,1536]{3,2,0,1:T(8,128)(2,1)} %copy.61), channel_id=1, source_target_pairs={{0,1},{1,0},{2,3},{3,2},{4,5},{5,4},{6,7},{7,6},{8,9},{9,8},{10,11... | collective-permute-start | bytes 3538952 | tf_op jit(solution)/shard_map/ppermute | solution.py:641
  427.3 35.5 %collective-permute-start.35 = (bf16[1,2,2,96,768]{4,3,2,1,0:T(8,128)(2,1)S(1)}, bf16[1,2,2,96,768]{4,3,2,1,0:T(8,128)(2,1)S(1)}, u32[]{:S(2)}, u32[]{:S(2)}) collective-permute-start(bf16[1,2,2,96,768]{4,3,2,1,0:T(8,128)(2,1)S(1)} %constant_dynamic-slice_fusion), channel_id=1, source_target_pairs={{0,8},{4,12},{8,0},{12,4},{1,9},{5,13},{9,1},{13,5},{2,10},{6,14},... | collective-permute-start | bytes 1769480 | tf_op jit(solution)/shard_map/ppermute | solution.py:641
  429.2 41.6 %collective-permute-start.30 = (bf16[4,48,1536]{2,1,0:T(8,128)(2,1)S(1)}, bf16[4,48,1536]{2,1,0:T(8,128)(2,1)S(1)}, u32[]{:S(2)}, u32[]{:S(2)}) collective-permute-start(bf16[4,48,1536]{2,1,0:T(8,128)(2,1)S(1)} %slice_bitcast_fusion), channel_id=1, source_target_pairs={{0,1},{1,0},{2,3},{3,2},{4,5},{5,4},{6,7},{7,6},{8,9},{9,8},{10,11... | collective-permute-start | bytes 1769480 | tf_op jit(solution)/shard_map/ppermute | solution.py:641
  433.8 25.3 %copy-start.3 = (bf16[1,384,1536]{2,1,0:T(8,128)(2,1)S(1)}, bf16[1,384,1536]{2,1,0:T(8,128)(2,1)}, u32[]{:S(2)}) copy-start(bf16[1,384,1536]{2,1,0:T(8,128)(2,1)} %get-tuple-element.125) | copy-start | bytes 3538948
  435.5 37.2 %collective-permute-start.25 = (bf16[4,1,48,1536]{3,2,0,1:T(8,128)(2,1)S(1)}, bf16[4,1,48,1536]{3,2,0,1:T(8,128)(2,1)S(1)}, u32[]{:S(2)}, u32[]{:S(2)}) collective-permute-start(bf16[4,1,48,1536]{3,2,0,1:T(8,128)(2,1)S(1)} %constant_dynamic-slice_fusion.3), channel_id=1, source_target_pairs={{0,2},{2,0},{1,3},{3,1},{4,6},{6,4},{5,7},{7,5},{8,10},{10,8},{9,1... | collective-permute-start | bytes 1769480 | tf_op jit(solution)/shard_map/ppermute | solution.py:641
  460.7 16.4 %collective-permute-start.20 = (bf16[4,1,48,1536]{3,2,0,1:T(8,128)(2,1)S(1)}, bf16[4,1,48,1536]{3,2,0,1:T(8,128)(2,1)S(1)}, u32[]{:S(2)}, u32[]{:S(2)}) collective-permute-start(bf16[4,1,48,1536]{3,2,0,1:T(8,128)(2,1)S(1)} %constant_dynamic-slice_fusion.5), channel_id=1, source_target_pairs={{0,2},{2,0},{1,3},{3,1},{4,6},{6,4},{5,7},{7,5},{8,10},{10,8},{9,1... | collective-permute-start | bytes 1769480 | tf_op jit(solution)/shard_map/ppermute | solution.py:641
  463.0 17.7 %collective-permute-start.36 = (bf16[1,2,96,768]{3,2,1,0:T(8,128)(2,1)S(1)}, bf16[1,2,96,768]{3,2,1,0:T(8,128)(2,1)S(1)}, u32[]{:S(2)}, u32[]{:S(2)}) collective-permute-start(bf16[1,2,96,768]{3,2,1,0:T(8,128)(2,1)S(1)} %dynamic-slice_bitcast_fusion.5), channel_id=1, source_target_pairs={{0,2},{2,0},{1,3},{3,1},{4,6},{6,4},{5,7},{7,5},{8,10},{10,8},{9,1... | collective-permute-start | bytes 884744 | tf_op jit(solution)/shard_map/ppermute | solution.py:641
  470.9 10.6 %collective-permute-start.31 = (bf16[2,48,1536]{2,1,0:T(8,128)(2,1)S(1)}, bf16[2,48,1536]{2,1,0:T(8,128)(2,1)S(1)}, u32[]{:S(2)}, u32[]{:S(2)}) collective-permute-start(bf16[2,48,1536]{2,1,0:T(8,128)(2,1)S(1)} %dynamic-slice_bitcast_fusion.6), channel_id=1, source_target_pairs={{0,4},{4,0},{8,12},{12,8},{1,5},{5,1},{9,13},{13,9},{2,6},{6,2},{1... | collective-permute-start | bytes 884744 | tf_op jit(solution)/shard_map/ppermute | solution.py:641
  472.9 18.8 %collective-permute-start.26 = (bf16[2,48,1536]{2,1,0:T(8,128)(2,1)S(1)}, bf16[2,48,1536]{2,1,0:T(8,128)(2,1)S(1)}, u32[]{:S(2)}, u32[]{:S(2)}) collective-permute-start(bf16[2,48,1536]{2,1,0:T(8,128)(2,1)S(1)} %dynamic-slice_bitcast_fusion.7), channel_id=1, source_target_pairs={{0,4},{4,0},{8,12},{12,8},{1,5},{5,1},{9,13},{13,9},{2,6},{6,2},{1... | collective-permute-start | bytes 884744 | tf_op jit(solution)/shard_map/ppermute | solution.py:641
  477.2 20.5 %collective-permute-start.21 = (bf16[2,48,1536]{2,1,0:T(8,128)(2,1)S(1)}, bf16[2,48,1536]{2,1,0:T(8,128)(2,1)S(1)}, u32[]{:S(2)}, u32[]{:S(2)}) collective-permute-start(bf16[2,48,1536]{2,1,0:T(8,128)(2,1)S(1)} %dynamic-slice_bitcast_fusion.8), channel_id=1, source_target_pairs={{0,4},{4,0},{8,12},{12,8},{1,5},{5,1},{9,13},{13,9},{2,6},{6,2},{1... | collective-permute-start | bytes 884744 | tf_op jit(solution)/shard_map/ppermute | solution.py:641
  480.9 24.2 %collective-permute-start.37 = (bf16[1,96,768]{2,1,0:T(8,128)(2,1)S(1)}, bf16[1,96,768]{2,1,0:T(8,128)(2,1)S(1)}, u32[]{:S(2)}, u32[]{:S(2)}) collective-permute-start(bf16[1,96,768]{2,1,0:T(8,128)(2,1)S(1)} %dynamic-slice_bitcast_fusion.9), channel_id=1, source_target_pairs={{0,1},{1,0},{2,3},{3,2},{4,5},{5,4},{6,7},{7,6},{8,9},{9,8},{10,11... | collective-permute-start | bytes 442376 | tf_op jit(solution)/shard_map/ppermute | solution.py:641
  481.6 16.3 %collective-permute-start.32 = (bf16[1,48,1536]{2,1,0:T(8,128)(2,1)S(1)}, bf16[1,48,1536]{2,1,0:T(8,128)(2,1)S(1)}, u32[]{:S(2)}, u32[]{:S(2)}) collective-permute-start(bf16[1,48,1536]{2,1,0:T(8,128)(2,1)S(1)} %constant_dynamic-slice_fusion.1), channel_id=1, source_target_pairs={{0,8},{4,12},{8,0},{12,4},{1,9},{5,13},{9,1},{13,5},{2,10},{6,14},... | collective-permute-start | bytes 442376 | tf_op jit(solution)/shard_map/ppermute | solution.py:641
  491.8 8.1 %collective-permute-start.27 = (bf16[1,48,1536]{2,1,0:T(8,128)(2,1)S(1)}, bf16[1,48,1536]{2,1,0:T(8,128)(2,1)S(1)}, u32[]{:S(2)}, u32[]{:S(2)}) collective-permute-start(bf16[1,48,1536]{2,1,0:T(8,128)(2,1)S(1)} %constant_dynamic-slice_fusion.2), channel_id=1, source_target_pairs={{0,8},{4,12},{8,0},{12,4},{1,9},{5,13},{9,1},{13,5},{2,10},{6,14},... | collective-permute-start | bytes 442376 | tf_op jit(solution)/shard_map/ppermute | solution.py:641
  497.9 6.5 %collective-permute-start.22 = (bf16[1,48,1536]{2,1,0:T(8,128)(2,1)S(1)}, bf16[1,48,1536]{2,1,0:T(8,128)(2,1)S(1)}, u32[]{:S(2)}, u32[]{:S(2)}) collective-permute-start(bf16[1,48,1536]{2,1,0:T(8,128)(2,1)S(1)} %constant_dynamic-slice_fusion.4), channel_id=1, source_target_pairs={{0,8},{4,12},{8,0},{12,4},{1,9},{5,13},{9,1},{13,5},{2,10},{6,14},... | collective-permute-start | bytes 442376 | tf_op jit(solution)/shard_map/ppermute | solution.py:641
  (11 other events, 47.3 us)
Sparse Core Ops, SparseCore 0:
  216.3 61.8 all-gather.3
